TPU v7x, 256 devices: a whole 4x4x8 slice. The times are simulated.
256 devices in a mesh: leaf: 32 (over z, x), agg: 2 (over core), probe: 4 (over y).
Axes of the slice: x: 4, y: 4, z: 8, core: 2. Of those that a mesh axis runs over, the one named last changes fastest.
Arguments:
- probes: float32 [4, 192, 8192], P('probe', None, ('leaf', 'agg')), may hold values from -16 to 16
- viscosity: float32 [192, 8192], P(None, ('leaf', 'agg')), may hold values from 0.1 to 10
- friction: float32 [192, 8192], P(None, ('leaf', 'agg')), may hold values from 0.05 to 1
- sensitivity: float32 [192, 8192], P(None, ('leaf', 'agg')), may hold values from 0.5 to 3
- misfit_weight: float32 [192, 8192], P(None, ('leaf', 'agg')), may hold values from 1 to 10
- grad_ref: float32 [192, 192], replicated, may hold values from -2 to 3, as said below
- trace_ref: float32 [192, 192], replicated, may hold values from -2 to 3
- coarse_modes: float32 [192, 128], replicated, may hold values from -0.4375 to 0.4375
- coarse_inv: float32 [512, 128, 128], P(('leaf', 'agg')), may hold values from -1 to 5, as said below
- peer_slots: int32 [64, 64, 16], P(('leaf', 'agg')), may hold values from -1 to 127, as said below
- local_pairs: int32 [2, 8192], P(None, ('leaf', 'agg')), may hold values from 0 to 127, as said below
- elem_agg: int32 [8192], P(('leaf', 'agg')), may hold values from 0 to 15
Outputs:
- incr_velocity: float32 [4, 192, 8192], P('probe', None, ('leaf', 'agg'))
- hess_action: float32 [4, 192, 8192], P('probe', None, ('leaf', 'agg'))
- trace_est: float32 [], replicated
Inputs may be any that keep to these rules, and one draw needn't show every extreme that they name: `grad_ref`: nonsingular. `coarse_inv`: each block is symmetric positive definite. peer_slots[P, Q, s] >= 0 exactly when peer_slots[Q, P, s] >= 0; the filled slots of a pair come first; no slot of a pair P, P is filled; the partitions are blocks of a three-dimensional grid and only blocks that touch by a face, edge or corner share slots, so a partition has at most 26 partners; some pair of partitions fills all 16 slots. `local_pairs`: the two elements of a pair differ.
All inputs are finite; a program needn't handle non-finite values.
Results may differ from a plain program's by a relative error of at most 0.0003.
Values sent between devices are 32-bit elements; how exact they have to be, the bound alone decides.
A program may use at most 64 MiB of HBM per device.

v0:
```python
import jax
import jax.numpy as jnp
from jax import lax
from jax.sharding import PartitionSpec as P

ITERS = 2
SWEEPS = 3


highest = lax.Precision.HIGHEST
relax_weight = 0.6


def matmul(left, right):
    return jnp.dot(left, right, precision=highest, preferred_element_type=jnp.float32)


def on_device(
    probes,
    viscosity,
    friction,
    sensitivity,
    misfit_weight,
    grad_ref,
    trace_ref,
    coarse_modes,
    coarse_inv,
    peer_slots,
    local_pairs,
    elem_agg,
):
    agg_count = lax.axis_size("agg")
    elem_local = viscosity.shape[1]
    slot_flat = peer_slots.reshape(-1)
    filled = slot_flat >= 0
    own_local = jnp.where(filled, slot_flat, 0)
    filled_float = filled.astype(jnp.float32)
    first_end = local_pairs[0]
    second_end = local_pairs[1]
    counts = jnp.zeros((elem_local,), jnp.float32)
    counts = counts.at[first_end].add(1.0).at[second_end].add(1.0).at[own_local].add(filled_float)
    trace_square = jnp.sum(trace_ref * trace_ref, axis=0)
    diag_op = (
        matmul((grad_ref * grad_ref).T, viscosity)
        + friction
        + counts[None, :] * trace_square[:, None]
    )
    group_aggs = agg_count * coarse_inv.shape[0]
    one_hot = (elem_agg[:, None] == jnp.arange(group_aggs, dtype=jnp.int32)[None, :]).astype(
        jnp.float32
    )

    def operate(field_vec):
        inner_term = matmul(grad_ref.T, viscosity * matmul(grad_ref, field_vec))
        traces = matmul(trace_ref, field_vec)
        outgoing = traces[:, own_local] * filled_float[None, :]
        incoming = lax.all_to_all(
            outgoing, ("leaf", "agg"), split_axis=1, concat_axis=1, tiled=True
        )
        cross_diff = outgoing - incoming
        local_diff = traces[:, first_end] - traces[:, second_end]
        accumulated = jnp.zeros_like(field_vec)
        accumulated = (
            accumulated.at[:, first_end].add(local_diff).at[:, second_end].add(-local_diff)
        )
        accumulated = accumulated.at[:, own_local].add(cross_diff)
        return inner_term + friction * field_vec + matmul(trace_ref.T, accumulated)

    def coarse(residual_now):
        projected = matmul(coarse_modes.T, residual_now)
        coarse_sums = matmul(projected, one_hot)
        own_sums = lax.psum_scatter(coarse_sums, "agg", scatter_dimension=1, tiled=True)
        solved_own = jnp.einsum("acd,da->ca", coarse_inv, own_sums, precision=highest)
        solved_all = lax.all_gather(solved_own, "agg", axis=1, tiled=True)
        return matmul(coarse_modes, matmul(solved_all, one_hot.T))

    def precond(residual_now):
        smooth = relax_weight * residual_now / diag_op
        for sweep_index in range(SWEEPS - 1):
            smooth = smooth + relax_weight * (residual_now - operate(smooth)) / diag_op
        return smooth + coarse(residual_now)

    def energy_sum(left, right):
        return lax.psum(jnp.sum(left * right), ("leaf", "agg"))

    def krylov(source):
        residual_now = source
        precon = precond(residual_now)
        search = precon
        energy_now = energy_sum(residual_now, precon)
        iterate = jnp.zeros_like(source)
        for iteration in range(ITERS):
            image_vec = operate(search)
            step_size = energy_now / lax.psum(jnp.sum(search * image_vec), ("leaf", "agg"))
            iterate = iterate + step_size * search
            if iteration + 1 < ITERS:
                residual_now = residual_now - step_size * image_vec
                precon = precond(residual_now)
                energy_next = energy_sum(residual_now, precon)
                search = precon + energy_next / energy_now * search
                energy_now = energy_next
        return iterate

    probe_field = probes[0]
    forward = krylov(sensitivity * probe_field)
    adjoint = krylov(misfit_weight * forward)
    action = sensitivity * adjoint
    trace_value = lax.psum(jnp.sum(probe_field * action), ("leaf", "agg", "probe")) / lax.axis_size(
        "probe"
    )
    return (forward[None], action[None], trace_value)


def solution(mesh):
    in_specs = (
        P("probe", None, ("leaf", "agg")),
        P(None, ("leaf", "agg")),
        P(None, ("leaf", "agg")),
        P(None, ("leaf", "agg")),
        P(None, ("leaf", "agg")),
        P(),
        P(),
        P(),
        P(("leaf", "agg"), None, None),
        P(("leaf", "agg"), None, None),
        P(None, ("leaf", "agg")),
        P(("leaf", "agg")),
    )
    out_specs = (P("probe", None, ("leaf", "agg")), P("probe", None, ("leaf", "agg")), P())
    return jax.shard_map(
        on_device, mesh=mesh, in_specs=in_specs, out_specs=out_specs, check_vma=False
    )
```

profile of v0, /device:TPU:8, one launch (start us, length us, event | category | flops | bytes accessed | tf_op | source)
XLA Modules:
  0.0 1492.4 jit_solution(4789891077508876401)
XLA Ops:
  20.2 12.2 all-to-all-start
  37.3 23.8 %all-to-all-done = f32[192,64,16]{0,2,1:T(8,128)} async-done(((f32[192,64,16]{0,2,1:T(8,128)}), f32[192,64,16]{0,2,1:T(8,128)}, u32[]{:S(2)}, u32[]{:S(2)}) %all-to-all-start) | async-done | bytes 786464 | tf_op jit(solution)/shard_map/all_to_all | solution.py:57
  62.5 9.0 scatter_custom_fusion.5
  100.6 12.8 all-to-all-done.1
  143.2 22.6 %all-to-all-done.2 = f32[192,64,16]{0,2,1:T(8,128)} async-done(((f32[192,64,16]{0,2,1:T(8,128)}), f32[192,64,16]{0,2,1:T(8,128)}, u32[]{:S(2)}, u32[]{:S(2)}) %all-to-all-start.2) | async-done | bytes 786464 | tf_op jit(solution)/shard_map/all_to_all | solution.py:57
  179.0 125.8 %all-reduce.5 = (f32[]{:T(128)}, f32[]{:T(128)}) all-reduce(f32[]{:T(128)} %get-tuple-element.6, f32[]{:T(128)} %get-tuple-element.5), channel_id=1, replica_groups=mesh['leaf'=32,'agg'=2,'probe'=4] {'leaf','agg'}, use_global_device_ids=true, to_apply=%region_12.13 | all-reduce | flops 2 | bytes 16 | tf_op jit(solution)/shard_map/psum | solution.py:84
  323.3 23.0 %all-to-all-done.3 = f32[192,64,16]{0,2,1:T(8,128)} async-done(((f32[192,64,16]{0,2,1:T(8,128)}), f32[192,64,16]{0,2,1:T(8,128)}, u32[]{:S(2)}, u32[]{:S(2)}) %all-to-all-start.3) | async-done | bytes 786464 | tf_op jit(solution)/shard_map/all_to_all | solution.py:57
  383.5 14.9 all-to-all-done.4
  399.9 9.0 scatter_custom_fusion.17
  412.1 125.8 %psum.65 = f32[]{:T(128)} all-reduce(f32[]{:T(128)} %get-tuple-element.20), channel_id=1, replica_groups=mesh['leaf'=32,'agg'=2,'probe'=4] {'leaf','agg'}, use_global_device_ids=true, to_apply=%region_26.27 | all-reduce | flops 1 | bytes 8 | tf_op jit(solution)/shard_map/psum | solution.py:84
  556.4 22.8 %all-to-all-done.5 = f32[192,64,16]{0,2,1:T(8,128)} async-done(((f32[192,64,16]{0,2,1:T(8,128)}), f32[192,64,16]{0,2,1:T(8,128)}, u32[]{:S(2)}, u32[]{:S(2)}) %all-to-all-start.5) | async-done | bytes 786464 | tf_op jit(solution)/shard_map/all_to_all | solution.py:57
  580.7 9.0 scatter_custom_fusion.20
  592.5 125.7 %psum.66 = f32[]{:T(128)} all-reduce(f32[]{:T(128)} %fusion.100), channel_id=1, replica_groups=mesh['leaf'=32,'agg'=2,'probe'=4] {'leaf','agg'}, use_global_device_ids=true, to_apply=%region_31.32 | all-reduce | flops 1 | bytes 8 | tf_op jit(solution)/shard_map/psum | solution.py:94
  737.2 23.0 %all-to-all-done.6 = f32[192,64,16]{0,2,1:T(8,128)} async-done(((f32[192,64,16]{0,2,1:T(8,128)}), f32[192,64,16]{0,2,1:T(8,128)}, u32[]{:S(2)}, u32[]{:S(2)}) %all-to-all-start.6) | async-done | bytes 786464 | tf_op jit(solution)/shard_map/all_to_all | solution.py:57
  761.7 9.0 scatter_custom_fusion.23
  797.7 14.9 all-to-all-done.7
  842.2 22.9 %all-to-all-done.8 = f32[192,64,16]{0,2,1:T(8,128)} async-done(((f32[192,64,16]{0,2,1:T(8,128)}), f32[192,64,16]{0,2,1:T(8,128)}, u32[]{:S(2)}, u32[]{:S(2)}) %all-to-all-start.8) | async-done | bytes 786464 | tf_op jit(solution)/shard_map/all_to_all | solution.py:57
  878.4 125.7 %all-reduce.4 = (f32[]{:T(128)}, f32[]{:T(128)}) all-reduce(f32[]{:T(128)} %get-tuple-element.4, f32[]{:T(128)} %get-tuple-element.3), channel_id=1, replica_groups=mesh['leaf'=32,'agg'=2,'probe'=4] {'leaf','agg'}, use_global_device_ids=true, to_apply=%region_40.41 | all-reduce | flops 2 | bytes 16 | tf_op jit(solution)/shard_map/psum | solution.py:84
  1022.4 23.1 %all-to-all-done.9 = f32[192,64,16]{0,2,1:T(8,128)} async-done(((f32[192,64,16]{0,2,1:T(8,128)}), f32[192,64,16]{0,2,1:T(8,128)}, u32[]{:S(2)}, u32[]{:S(2)}) %all-to-all-start.9) | async-done | bytes 786464 | tf_op jit(solution)/shard_map/all_to_all | solution.py:57
  1082.7 14.9 all-to-all-done.10
  1111.3 125.7 %psum.69 = f32[]{:T(128)} all-reduce(f32[]{:T(128)} %get-tuple-element.23), channel_id=1, replica_groups=mesh['leaf'=32,'agg'=2,'probe'=4] {'leaf','agg'}, use_global_device_ids=true, to_apply=%region_54.55 | all-reduce | flops 1 | bytes 8 | tf_op jit(solution)/shard_map/psum | solution.py:84
  1258.4 19.8 %all-to-all-done.11 = f32[192,64,16]{0,2,1:T(8,128)S(1)} async-done(((f32[192,64,16]{0,2,1:T(8,128)}), f32[192,64,16]{0,2,1:T(8,128)S(1)}, u32[]{:S(2)}, u32[]{:S(2)}) %all-to-all-start.11) | async-done | bytes 786464 | tf_op jit(solution)/shard_map/all_to_all | solution.py:57
  1289.3 125.7 %psum.70 = f32[]{:T(128)} all-reduce(f32[]{:T(128)} %fusion.99), channel_id=1, replica_groups=mesh['leaf'=32,'agg'=2,'probe'=4] {'leaf','agg'}, use_global_device_ids=true, to_apply=%region_59.60 | all-reduce | flops 1 | bytes 8 | tf_op jit(solution)/shard_map/psum | solution.py:94
  1417.6 72.5 %psum.71 = f32[]{:T(128)} all-reduce(f32[]{:T(128)} %get-tuple-element.11), channel_id=1, replica_groups=mesh['leaf'=32,'agg'=2,'probe'=4] {'leaf','agg','probe'}, use_global_device_ids=true, to_apply=%region_61.62 | all-reduce | flops 1 | bytes 8 | tf_op jit(solution)/shard_map/psum | solution.py:108
  (347 shorter events, 365.7 us)
Async XLA Ops:
  0.6 90.6 %copy-start = (f32[8,128,128]{2,1,0:T(8,128)S(1)}, f32[8,128,128]{2,1,0:T(8,128)}, u32[]{:S(2)}) copy-start(f32[8,128,128]{2,1,0:T(8,128)} %param.20) | copy-start | bytes 1572868
  2.6 31.4 %copy-start.59 = (s32[128]{0:T(128)}, s32[128]{0:T(128)S(1)}, u32[]{:S(2)}) copy-start(s32[128]{0:T(128)S(1)} %get-tuple-element.18) | copy-start | bytes 1540
  2.6 32.7 %copy-start.58 = (s32[128]{0:T(128)}, s32[128]{0:T(128)S(1)}, u32[]{:S(2)}) copy-start(s32[128]{0:T(128)S(1)} %get-tuple-element.17) | copy-start | bytes 1540
  20.2 40.9 %all-to-all-start = ((f32[192,64,16]{0,2,1:T(8,128)}), f32[192,64,16]{0,2,1:T(8,128)}, u32[]{:S(2)}, u32[]{:S(2)}) async-start(f32[192,64,16]{0,2,1:T(8,128)} %broadcast_multiply_fusion.11), calls=%async_computation | async-start | bytes 2097152 | tf_op jit(solution)/shard_map/all_to_all | solution.py:57
  73.6 26.0 %copy-start.15 = (f32[192,128]{1,0:T(8,128)}, f32[192,128]{1,0:T(8,128)S(1)}, u32[]{:S(2)}) copy-start(f32[192,128]{1,0:T(8,128)S(1)} %fusion.74) | copy-start | bytes 294916
  78.7 34.6 %all-to-all-start.1 = ((f32[192,64,16]{0,2,1:T(8,128)}), f32[192,64,16]{0,2,1:T(8,128)}, u32[]{:S(2)}, u32[]{:S(2)}) async-start(f32[192,64,16]{0,2,1:T(8,128)} %broadcast_multiply_fusion.10), calls=%async_computation.1 | async-start | bytes 2097152 | tf_op jit(solution)/shard_map/all_to_all | solution.py:57
  131.6 34.2 %all-to-all-start.2 = ((f32[192,64,16]{0,2,1:T(8,128)}), f32[192,64,16]{0,2,1:T(8,128)}, u32[]{:S(2)}, u32[]{:S(2)}) async-start(f32[192,64,16]{0,2,1:T(8,128)} %broadcast_multiply_fusion.9), calls=%async_computation.2 | async-start | bytes 2097152 | tf_op jit(solution)/shard_map/all_to_all | solution.py:57
  311.4 35.0 %all-to-all-start.3 = ((f32[192,64,16]{0,2,1:T(8,128)}), f32[192,64,16]{0,2,1:T(8,128)}, u32[]{:S(2)}, u32[]{:S(2)}) async-start(f32[192,64,16]{0,2,1:T(8,128)} %broadcast_multiply_fusion.8), calls=%async_computation.3 | async-start | bytes 2097152 | tf_op jit(solution)/shard_map/all_to_all | solution.py:57
  364.0 34.4 %all-to-all-start.4 = ((f32[192,64,16]{0,2,1:T(8,128)}), f32[192,64,16]{0,2,1:T(8,128)}, u32[]{:S(2)}, u32[]{:S(2)}) async-start(f32[192,64,16]{0,2,1:T(8,128)} %broadcast_multiply_fusion.7), calls=%async_computation.4 | async-start | bytes 2097152 | tf_op jit(solution)/shard_map/all_to_all | solution.py:57
  411.3 127.9 %copy-start.12 = (f32[192,128]{1,0:T(8,128)S(1)}, f32[192,128]{1,0:T(8,128)}, u32[]{:S(2)}) copy-start(f32[192,128]{1,0:T(8,128)} %copy-done.10) | copy-start | bytes 294916
  544.4 34.9 %all-to-all-start.5 = ((f32[192,64,16]{0,2,1:T(8,128)}), f32[192,64,16]{0,2,1:T(8,128)}, u32[]{:S(2)}, u32[]{:S(2)}) async-start(f32[192,64,16]{0,2,1:T(8,128)} %broadcast_multiply_fusion.6), calls=%async_computation.5 | async-start | bytes 2097152 | tf_op jit(solution)/shard_map/all_to_all | solution.py:57
  591.2 128.1 %copy-start.13 = (f32[192,128]{1,0:T(8,128)S(1)}, f32[192,128]{1,0:T(8,128)}, u32[]{:S(2)}) copy-start(f32[192,128]{1,0:T(8,128)} %copy-done.10) | copy-start | bytes 294916
  591.3 128.1 %copy-start.53 = (f32[192,128]{1,0:T(8,128)S(1)}, f32[192,128]{1,0:T(8,128)}, u32[]{:S(2)}) copy-start(f32[192,128]{1,0:T(8,128)} %param.16) | copy-start | bytes 294916
  725.2 35.1 %all-to-all-start.6 = ((f32[192,64,16]{0,2,1:T(8,128)}), f32[192,64,16]{0,2,1:T(8,128)}, u32[]{:S(2)}, u32[]{:S(2)}) async-start(f32[192,64,16]{0,2,1:T(8,128)} %broadcast_multiply_fusion.5), calls=%async_computation.6 | async-start | bytes 2097152 | tf_op jit(solution)/shard_map/all_to_all | solution.py:57
  772.8 23.9 %copy-start.21 = (f32[192,128]{1,0:T(8,128)}, f32[192,128]{1,0:T(8,128)S(1)}, u32[]{:S(2)}) copy-start(f32[192,128]{1,0:T(8,128)S(1)} %fusion.62) | copy-start | bytes 294916
  778.0 34.7 %all-to-all-start.7 = ((f32[192,64,16]{0,2,1:T(8,128)}), f32[192,64,16]{0,2,1:T(8,128)}, u32[]{:S(2)}, u32[]{:S(2)}) async-start(f32[192,64,16]{0,2,1:T(8,128)} %broadcast_multiply_fusion.4), calls=%async_computation.7 | async-start | bytes 2097152 | tf_op jit(solution)/shard_map/all_to_all | solution.py:57
  830.9 34.2 %all-to-all-start.8 = ((f32[192,64,16]{0,2,1:T(8,128)}), f32[192,64,16]{0,2,1:T(8,128)}, u32[]{:S(2)}, u32[]{:S(2)}) async-start(f32[192,64,16]{0,2,1:T(8,128)} %broadcast_multiply_fusion.3), calls=%async_computation.8 | async-start | bytes 2097152 | tf_op jit(solution)/shard_map/all_to_all | solution.py:57
  1010.5 34.9 %all-to-all-start.9 = ((f32[192,64,16]{0,2,1:T(8,128)}), f32[192,64,16]{0,2,1:T(8,128)}, u32[]{:S(2)}, u32[]{:S(2)}) async-start(f32[192,64,16]{0,2,1:T(8,128)} %broadcast_multiply_fusion.2), calls=%async_computation.9 | async-start | bytes 2097152 | tf_op jit(solution)/shard_map/all_to_all | solution.py:57
  1063.2 34.5 %all-to-all-start.10 = ((f32[192,64,16]{0,2,1:T(8,128)}), f32[192,64,16]{0,2,1:T(8,128)}, u32[]{:S(2)}, u32[]{:S(2)}) async-start(f32[192,64,16]{0,2,1:T(8,128)} %broadcast_multiply_fusion.1), calls=%async_computation.10 | async-start | bytes 2097152 | tf_op jit(solution)/shard_map/all_to_all | solution.py:57
  1110.4 127.9 %copy-start.8 = (f32[192,128]{1,0:T(8,128)S(1)}, f32[192,128]{1,0:T(8,128)}, u32[]{:S(2)}) copy-start(f32[192,128]{1,0:T(8,128)} %copy-done.6) | copy-start | bytes 294916
  1243.5 34.8 %all-to-all-start.11 = ((f32[192,64,16]{0,2,1:T(8,128)}), f32[192,64,16]{0,2,1:T(8,128)S(1)}, u32[]{:S(2)}, u32[]{:S(2)}) async-start(f32[192,64,16]{0,2,1:T(8,128)} %broadcast_multiply_fusion), calls=%async_computation.11 | async-start | bytes 2097152 | tf_op jit(solution)/shard_map/all_to_all | solution.py:57
  1288.1 128.2 %copy-start.9 = (f32[192,128]{1,0:T(8,128)S(1)}, f32[192,128]{1,0:T(8,128)}, u32[]{:S(2)}) copy-start(f32[192,128]{1,0:T(8,128)} %copy-done.6) | copy-start | bytes 294916
  1288.1 128.2 %copy-start.36 = (f32[192,128]{1,0:T(8,128)S(1)}, f32[192,128]{1,0:T(8,128)}, u32[]{:S(2)}) copy-start(f32[192,128]{1,0:T(8,128)} %param.15) | copy-start | bytes 294916
  1288.1 128.2 %copy-start.38 = (f32[1,192,128]{2,1,0:T(8,128)S(1)}, f32[1,192,128]{2,1,0:T(8,128)}, u32[]{:S(2)}) copy-start(f32[1,192,128]{2,1,0:T(8,128)} %param.12) | copy-start | bytes 294916
  (50 other events, 179.0 us)
where the time goes:
time: 1510 us; the launch traced here: 1490 us
  blocking collectives  849 us (56%)
  waiting for transfers between devices  239 us (16%)
  other arithmetic  191 us (13%)
  starting transfers between devices  77.3 us (5%)
  local copies, waits for them, and re-layouts  70.4 us (5%)
  matrix products  54 us (4%)
    psum x4, blocking collectives, energy_sum(): return lax.psum(jnp.sum(left * right), ('leaf', 'agg'))  503 us
    psum x2, blocking collectives, krylov(): lax.psum(jnp.sum(search * image_vec), ('leaf', 'agg'))  251 us
    all_to_all x12, waiting for transfers between devices, operate(): lax.all_to_all(outgoing, ('leaf', 'agg'), split_axis=1, concat_axis=1, ti...  239 us
    scatter-add x12, other arithmetic, operate(): accumulated = accumulated.at[:, own_local].add(cross_diff)  107 us
    all_to_all x12, starting transfers between devices, operate(): lax.all_to_all(outgoing, ('leaf', 'agg'), split_axis=1, concat_axis=1, ti...  77.3 us
    psum x1, blocking collectives, on_device(): lax.psum(jnp.sum(probe_field * action), ('leaf', 'agg', 'probe'))  72.5 us
    dot_general x65, matrix products, matmul(): jnp.dot(left, right, precision=highest, preferred_element_type=jnp.float32)  50.2 us
    gather x12, local copies, waits for them, and re-layouts, operate(): outgoing = traces[:, own_local] * filled_float[None, :]  41.6 us
  transfers between devices with their start and end apart: 12, of which 12 were waited for; matrix products, arithmetic and copies ran while one was open for 5% of the time, Pallas kernels for 0%

commit v1 on v0

v1 whole, which is shorter than its diff:
```python
import functools
import jax
import jax.numpy as jnp
from jax import lax
from jax.experimental import pallas as pl
from jax.experimental.pallas import tpu as pltpu
from jax.sharding import PartitionSpec as P

MESH = pl.DeviceIdType.MESH
F32 = jnp.float32
BF16 = jnp.bfloat16
AXES = ("leaf", "agg", "probe")
RELAX = 0.6
CAP = 16
NT = (((1,), (1,)), ((), ()))
X = 4

RELOCATE = True


def split(value):
    high = value.astype(BF16)
    return high, (value - high.astype(F32)).astype(BF16)


def dot(left, right):
    return jnp.dot(left, right, preferred_element_type=F32)


def dot_exact(left, right_pair):
    return dot(left, right_pair[0]) + dot(left, right_pair[1])


def dot_split(left, right_pair):
    left_high, left_low = split(left)
    return dot(left_high, right_pair[0]) + (
        dot(left_low, right_pair[0]) + dot(left_high, right_pair[1])
    )


def place(unit, probe, probes):
    leaf, agg = unit // 2, unit % 2
    if not RELOCATE:
        return leaf, agg, probe
    z, x = leaf // X, leaf % X
    pair = leaf_pair(probes)
    return (probe * pair + z % pair) * X + x, agg, z // pair


def leaf_pair(probes):
    return 2


def kernel(
    parts,
    probes,
    fields,
    grad,
    trace,
    modes,
    inv,
    ints,
    out,
    trace_out,
    weights_h,
    weights_l,
    modes_h,
    modes_l,
    modes_t_h,
    modes_t_l,
    inv_h,
    inv_l,
    scatter,
    scatter_two,
    gather,
    gather_two,
    adjacent,
    group_sum,
    group_spread,
    visc,
    fric,
    misfit,
    inv_diag,
    count,
    probe_sens,
    rhs,
    first_dir,
    image,
    pre,
    traces,
    send,
    recv,
    sums,
    sums_in,
    solved,
    dots_a,
    dots_b,
    traces_all,
    send_sem,
    recv_sem,
    coarse_send_sem,
    coarse_recv_sem,
    dots_send_sem,
    dots_recv_sem,
    last_send_sem,
    last_recv_sem,
):
    leaf, agg, along = lax.axis_index("leaf"), lax.axis_index("agg"), lax.axis_index("probe")
    if RELOCATE:
        z, x = leaf // X, leaf % X
        probe = z // 2
        unit = ((along * 2 + z % 2) * X + x) * 2 + agg
    else:
        probe = along
        unit = leaf * 2 + agg
    sibling = (leaf, 1 - agg, along)
    ndof = grad.shape[0]
    elems = fields.shape[2]
    halves = CAP // 2
    others = parts - 1

    def partner(step):
        return lax.rem(unit + step, parts)

    barrier = pltpu.get_barrier_semaphore()

    @pl.loop(1, parts)
    def _(step):
        pl.semaphore_signal(
            barrier, inc=1, device_id=place(partner(step), probe, probes), device_id_type=MESH
        )

    @pl.loop(1, probes)
    def _(step):
        pl.semaphore_signal(
            barrier,
            inc=1,
            device_id=place(unit, lax.rem(probe + step, probes), probes),
            device_id_type=MESH,
        )

    for slot, matrix in enumerate((grad[...].T, grad[...], trace[...].T, trace[...])):
        weights_h[slot], weights_l[slot] = split(matrix)
    modes_h[...], modes_l[...] = split(modes[...])
    modes_t_h[...], modes_t_l[...] = split(modes[...].T)
    for block in range(inv.shape[0]):
        inv_h[block], inv_l[block] = split(inv[block])
    rows = lax.broadcasted_iota(jnp.int32, (elems, elems), 0).astype(F32)

    def one_hot(row):
        return (ints[pl.ds(row, 1), :] == rows).astype(F32)

    slots = parts * CAP
    cross = jnp.zeros((elems, 1), F32)
    for block in range(slots // elems):
        hot = one_hot(block)
        cross = cross + jnp.sum(hot, axis=1, keepdims=True)
        here = pl.ds(block * elems, elems)
        scatter[:, here] = hot.astype(BF16)
        hot_t = hot.T
        gather[here, :] = hot_t.astype(BF16)
        paired = hot_t.reshape(elems // CAP, 2, halves, elems)
        low = paired[:, 0].reshape(elems // 2, elems)
        high = paired[:, 1].reshape(elems // 2, elems)
        half = pl.ds(block * (elems // 2), elems // 2)
        gather_two[half, :elems] = low.astype(BF16)
        gather_two[half, elems:] = high.astype(BF16)
    for block in range(slots // elems // 2):
        here = pl.ds(block * elems, elems)
        scatter_two[:elems, here] = gather_two[here, :elems].astype(F32).T.astype(BF16)
        scatter_two[elems:, here] = gather_two[here, elems:].astype(F32).T.astype(BF16)
    base = slots // elems
    ends = [one_hot(base + end).astype(BF16) for end in range(2)]
    near = lax.dot_general(ends[0], ends[1], NT, preferred_element_type=F32)
    near = near + lax.dot_general(ends[1], ends[0], NT, preferred_element_type=F32)
    adjacent[...] = near.astype(BF16)
    count[...] = cross + jnp.sum(near, axis=1, keepdims=True)
    hot = one_hot(base + 2)
    group_sum[...] = hot[: sums.shape[0]].astype(BF16)
    group_spread[...] = hot.T.astype(BF16)

    visc[...] = fields[1].T
    fric[...] = fields[2].T
    misfit[...] = fields[4].T
    square = grad[...] * grad[...]
    trace_square = jnp.sum(trace[...] * trace[...], axis=0, keepdims=True)
    diag = dot_split(visc[...], split(square)) + fric[...] + count[...] * trace_square
    inv_diag[...] = RELAX / diag
    start = (fields[3] * fields[0]).T
    probe_sens[...] = start
    rhs[...] = start
    solved[...] = jnp.zeros_like(solved)
    for turn in range(2):
        recv[turn, unit] = jnp.zeros(recv.shape[2:], F32)
    pl.semaphore_wait(barrier, others + probes - 1)

    def weight(slot):
        return weights_h[slot], weights_l[slot]

    def block_copy(turn, peer):
        return pltpu.make_async_remote_copy(
            src_ref=send.at[turn, peer],
            dst_ref=recv.at[turn, unit],
            send_sem=send_sem.at[turn],
            recv_sem=recv_sem.at[turn],
            device_id=place(peer, probe, probes),
            device_id_type=MESH,
        )

    def wait_blocks(turn, sem):
        blocks = recv.at[turn, pl.ds(0, others)]
        pltpu.make_async_copy(blocks, blocks, sem.at[turn]).wait()

    def operate(value, turn):
        traced = dot_split(value, weight(2))
        high, low = split(traced)
        blank = jnp.zeros((elems, 2 * elems - ndof), BF16)
        send[turn, :, :CAP, :] = dot_exact(
            gather[...], (high[:, :elems], low[:, :elems])
        ).reshape(parts, CAP, elems)

        def two(piece):
            rest = piece[:, elems:]
            return jnp.concatenate(
                [jnp.concatenate([rest, blank], 1), jnp.concatenate([blank, rest], 1)], 0
            )

        send[turn, :, CAP:, :] = dot_exact(gather_two[...], (two(high), two(low))).reshape(
            parts, halves, elems
        )

        @pl.loop(1, parts)
        def _(step):
            block_copy(turn, partner(step)).start()

        inner = dot_split(visc[...] * dot_split(value, weight(0)), weight(1))
        near = count[...] * traced - dot_exact(adjacent[...], (high, low))
        inner = inner + fric[...] * value
        wait_blocks(turn, recv_sem)
        first = dot_exact(scatter[...], split(recv[turn, :, :CAP, :].reshape(slots, elems)))
        second = dot_exact(
            scatter_two[...], split(recv[turn, :, CAP:, :].reshape(slots // 2, elems))
        )
        rest = 2 * elems - ndof
        second = second[:elems, :rest] + second[elems:, rest:]
        near = near - jnp.concatenate([first, second], 1)
        result = inner + dot_split(near, weight(3))
        wait_blocks(turn, send_sem)
        return result

    own_rows = pl.ds(pl.multiple_of(agg * 8, 8), 8)
    peer_rows = pl.ds(pl.multiple_of((1 - agg) * 8, 8), 8)
    sums_copy = pltpu.make_async_remote_copy(
        src_ref=sums.at[peer_rows],
        dst_ref=sums_in,
        send_sem=coarse_send_sem.at[0],
        recv_sem=coarse_recv_sem.at[0],
        device_id=sibling,
        device_id_type=MESH,
    )
    solved_copy = pltpu.make_async_remote_copy(
        src_ref=solved.at[own_rows],
        dst_ref=solved.at[own_rows],
        send_sem=coarse_send_sem.at[1],
        recv_sem=coarse_recv_sem.at[1],
        device_id=sibling,
        device_id_type=MESH,
    )

    def coarse_start(residual):
        projected = dot_split(residual, (modes_h[...], modes_l[...]))
        sums[...] = dot_exact(group_sum[...], split(projected))
        sums_copy.start()

    def coarse_solve():
        sums_copy.wait()
        total = sums[own_rows, :] + sums_in[...]
        row = lax.broadcasted_iota(jnp.int32, total.shape, 0)
        result = jnp.zeros_like(total)
        for block in range(total.shape[0]):
            one = dot_split(total, (inv_h[block], inv_l[block]))
            result = jnp.where(row == block, one, result)
        solved[own_rows, :] = result
        solved_copy.start()

    def coarse_end():
        solved_copy.wait()
        spread = dot_exact(group_spread[...], split(solved[...]))
        return dot_split(spread, (modes_t_h[...], modes_t_l[...]))

    def precondition(residual_ref, turn):
        residual = residual_ref[...]
        coarse_start(residual)
        pre[...] = residual * inv_diag[...]
        pre[...] += (residual_ref[...] - operate(pre[...], turn)) * inv_diag[...]
        coarse_solve()
        pre[...] += (residual_ref[...] - operate(pre[...], 1 - turn)) * inv_diag[...]
        return pre[...] + coarse_end()

    def lanes(left, right):
        total = jnp.sum(left * right, axis=0, keepdims=True)
        tail = jnp.concatenate(
            [total[:, elems:], jnp.zeros((1, 2 * elems - ndof), F32)], 1
        )
        return total[:, :elems] + tail

    def dots_copy(buffer, which, peer):
        return pltpu.make_async_remote_copy(
            src_ref=buffer.at[unit],
            dst_ref=buffer.at[unit],
            send_sem=dots_send_sem.at[which],
            recv_sem=dots_recv_sem.at[which],
            device_id=place(peer, probe, probes),
            device_id_type=MESH,
        )

    def dots_start(buffer, which, pieces):
        pad = 8 - len(pieces)
        buffer[unit] = jnp.concatenate(list(pieces) + [jnp.zeros((pad, elems), F32)], 0)

        @pl.loop(1, parts)
        def _(step):
            dots_copy(buffer, which, partner(step)).start()

    def dots_end(buffer, which):
        blocks = buffer.at[pl.ds(0, others)]
        pltpu.make_async_copy(blocks, blocks, dots_recv_sem.at[which]).wait()
        pltpu.make_async_copy(blocks, blocks, dots_send_sem.at[which]).wait()
        total = jnp.sum(jnp.sum(buffer[...], axis=0), axis=1, keepdims=True)
        return [total[row : row + 1] for row in range(8)]

    @pl.loop(0, 2)
    def _(solve):
        first_dir[...] = precondition(rhs, 0)
        image[...] = operate(first_dir[...], 0)
        dots_start(
            dots_a,
            0,
            [lanes(rhs[...], first_dir[...]), lanes(first_dir[...], image[...])],
        )
        second = precondition(image, 1)
        energy, curve, *_ = dots_end(dots_a, 0)
        step = energy / curve
        second = first_dir[...] - step * second
        residual = rhs[...] - step * image[...]
        pre[...] = second
        second_image = operate(pre[...], 1)
        second = pre[...]
        dots_start(
            dots_b,
            1,
            [
                lanes(residual, second),
                lanes(second, second_image),
                lanes(second, image[...]),
                lanes(probe_sens[...], first_dir[...]),
                lanes(probe_sens[...], second),
            ],
        )
        energy_next, curve_zz, curve_zp, trace_first, trace_second, *_ = dots_end(dots_b, 1)
        ratio = energy_next / energy
        curve_next = curve_zz + 2.0 * ratio * curve_zp + ratio * ratio * curve
        step_next = energy_next / curve_next
        weight_first = step + step_next * ratio
        result = weight_first * first_dir[...] + step_next * pre[...]
        rhs[...] = misfit[...] * result
        out[solve] = result.T
        value = weight_first * trace_first + step_next * trace_second
        traces[...] = jnp.broadcast_to(value, traces.shape)

    out[1] = out[1] * fields[3]
    traces_all[probe] = traces[...]

    def last_copy(step):
        return pltpu.make_async_remote_copy(
            src_ref=traces,
            dst_ref=traces_all.at[probe],
            send_sem=last_send_sem,
            recv_sem=last_recv_sem,
            device_id=place(unit, lax.rem(probe + step, probes), probes),
            device_id_type=MESH,
        )

    @pl.loop(1, probes)
    def _(step):
        last_copy(step).start()

    blocks = traces_all.at[pl.ds(0, probes - 1)]
    pltpu.make_async_copy(blocks, blocks, last_recv_sem).wait()
    pltpu.make_async_copy(blocks, blocks, last_send_sem).wait()
    trace_out[...] = jnp.sum(traces_all[...], axis=0) / probes


def on_device(
    probes,
    viscosity,
    friction,
    sensitivity,
    misfit_weight,
    grad_ref,
    trace_ref,
    coarse_modes,
    coarse_inv,
    peer_slots,
    local_pairs,
    elem_agg,
):
    leaves, aggs, count = (lax.axis_size(axis) for axis in AXES)
    parts = leaves * aggs
    ndof, elems = viscosity.shape
    own_aggs, modes_n = coarse_inv.shape[:2]
    slots = parts * CAP
    ints = jnp.concatenate(
        [
            peer_slots.reshape(slots // elems, elems),
            local_pairs,
            elem_agg[None],
            jnp.zeros((5, elems), jnp.int32),
        ]
    ).astype(F32)
    fields = jnp.stack([probes[0], viscosity, friction, sensitivity, misfit_weight])
    if RELOCATE:
        moves = []
        for unit in range(parts):
            for probe in range(count):
                leaf, agg, along = place(unit, probe, count)
                moves.append((unit * count + probe, (leaf * aggs + agg) * count + along))
        back = [(to, source) for source, to in moves]
        fields = lax.ppermute(fields, AXES, moves)
        ints = lax.ppermute(ints, AXES, moves)
        coarse_inv = lax.ppermute(coarse_inv, AXES, moves)

    def vmem(*shape, dtype=F32):
        return pltpu.VMEM(shape, dtype)

    field = vmem(elems, ndof)
    scratch = [
        vmem(4, ndof, ndof, dtype=BF16),
        vmem(4, ndof, ndof, dtype=BF16),
        vmem(ndof, modes_n, dtype=BF16),
        vmem(ndof, modes_n, dtype=BF16),
        vmem(modes_n, ndof, dtype=BF16),
        vmem(modes_n, ndof, dtype=BF16),
        vmem(own_aggs, modes_n, modes_n, dtype=BF16),
        vmem(own_aggs, modes_n, modes_n, dtype=BF16),
        vmem(elems, slots, dtype=BF16),
        vmem(2 * elems, slots // 2, dtype=BF16),
        vmem(slots, elems, dtype=BF16),
        vmem(slots // 2, 2 * elems, dtype=BF16),
        vmem(elems, elems, dtype=BF16),
        vmem(aggs * own_aggs, elems, dtype=BF16),
        vmem(elems, elems, dtype=BF16),
        field,
        field,
        field,
        field,
        vmem(elems, 1),
        field,
        field,
        field,
        field,
        field,
        vmem(8, elems),
        vmem(2, parts, CAP + CAP // 2, elems),
        vmem(2, parts, CAP + CAP // 2, elems),
        vmem(aggs * own_aggs, modes_n),
        vmem(own_aggs, modes_n),
        vmem(elems, modes_n),
        vmem(parts, 8, elems),
        vmem(parts, 8, elems),
        vmem(count, 8, elems),
        pltpu.SemaphoreType.DMA((2,)),
        pltpu.SemaphoreType.DMA((2,)),
        pltpu.SemaphoreType.DMA((2,)),
        pltpu.SemaphoreType.DMA((2,)),
        pltpu.SemaphoreType.DMA((2,)),
        pltpu.SemaphoreType.DMA((2,)),
        pltpu.SemaphoreType.DMA,
        pltpu.SemaphoreType.DMA,
    ]
    out, trace_tile = pl.pallas_call(
        functools.partial(kernel, parts, count),
        out_shape=(
            jax.ShapeDtypeStruct((2, ndof, elems), F32),
            jax.ShapeDtypeStruct((8, elems), F32),
        ),
        in_specs=[pl.BlockSpec(memory_space=pltpu.VMEM)] * 6,
        out_specs=(pl.BlockSpec(memory_space=pltpu.VMEM),) * 2,
        scratch_shapes=scratch,
        compiler_params=pltpu.CompilerParams(
            collective_id=0, has_side_effects=True, vmem_limit_bytes=48 * 1024 * 1024
        ),
    )(fields, grad_ref, trace_ref, coarse_modes, coarse_inv, ints)
    if RELOCATE:
        out = lax.ppermute(out, AXES, back)
    return out[0][None], out[1][None], trace_tile[0, 0]


def solution(mesh):
    in_specs = (
        P("probe", None, ("leaf", "agg")),
        P(None, ("leaf", "agg")),
        P(None, ("leaf", "agg")),
        P(None, ("leaf", "agg")),
        P(None, ("leaf", "agg")),
        P(),
        P(),
        P(),
        P(("leaf", "agg"), None, None),
        P(("leaf", "agg"), None, None),
        P(None, ("leaf", "agg")),
        P(("leaf", "agg")),
    )
    out_specs = (P("probe", None, ("leaf", "agg")), P("probe", None, ("leaf", "agg")), P())
    return jax.shard_map(
        on_device, mesh=mesh, in_specs=in_specs, out_specs=out_specs, check_vma=False
    )
```

time: 1510 us -> 307 us (0.20); the launches traced: 1490 us -> 307 us
  blocking collectives: 849 us -> 0 us
  Pallas kernels: 0 us -> 214 us
  other arithmetic: 191 us -> 0.07 us
  waiting for transfers between devices: 239 us -> 69 us
  local copies, waits for them, and re-layouts: 70.4 us -> 4.81 us
  starting transfers between devices: 77.3 us -> 17.5 us
  matrix products: 54 us -> 0 us
    psum x7 -> x0, blocking collectives: 827 us -> none  [the longest x4 503 us: energy_sum(): return lax.psum(jnp.sum(left * right), ('leaf', 'agg'))]
    all_to_all x12 -> x0, waiting for transfers between devices: 239 us -> none  [operate(): lax.all_to_all(outgoing, ('leaf', 'agg'), split_axis=1, concat_axis=1, ti...]
    pallas_call x0 -> x1, Pallas kernels: none -> 214 us  [on_device(): pl.pallas_call(functools.partial(kernel, parts, count), out_shape=(jax.Sh...]
    scatter-add x39 -> x0, other arithmetic: 156 us -> none  [the longest x12 107 us: operate(): accumulated = accumulated.at[:, own_local].add(cross_diff)]
    all_to_all x12 -> x0, starting transfers between devices: 77.3 us -> none  [operate(): lax.all_to_all(outgoing, ('leaf', 'agg'), split_axis=1, concat_axis=1, ti...]
    ppermute x0 -> x4, waiting for transfers between devices: none -> 69 us  [the longest x1 55.6 us: on_device(): ints = lax.ppermute(ints, AXES, moves)]
    gather x36 -> x0, local copies, waits for them, and re-layouts: 63.6 us -> none  [the longest x12 41.6 us: operate(): outgoing = traces[:, own_local] * filled_float[None, :]]
    dot_general x69 -> x0, matrix products: 54 us -> none  [the longest x65 50.2 us: matmul(): jnp.dot(left, right, precision=highest, preferred_element_type=jnp.float32)]
  transfers between devices with their start and end apart: 12 -> 4, of which waited for: 12 -> 2; matrix products, arithmetic and copies ran while one was open for 5% -> 1% of each run, Pallas kernels for 0% -> 0%
where the time goes in v1:
time: 307 us
  Pallas kernels  214 us (70%)
  waiting for transfers between devices  69 us (22%)
  starting transfers between devices  17.5 us (6%)
  local copies, waits for them, and re-layouts  4.81 us (2%)
    pallas_call x1, Pallas kernels, on_device(): pl.pallas_call(functools.partial(kernel, parts, count), out_shape=(jax.Sh...  214 us
    ppermute x1, waiting for transfers between devices, on_device(): ints = lax.ppermute(ints, AXES, moves)  55.6 us
    ppermute x1, waiting for transfers between devices, on_device(): out = lax.ppermute(out, AXES, back)  13.5 us
  transfers between devices with their start and end apart: 4, of which 2 were waited for; matrix products, arithmetic and copies ran while one was open for 1% of the time, Pallas kernels for 0%

profile of v1, /device:TPU:8, one launch (start us, length us, event | category | flops | bytes accessed | tf_op | source)
XLA Modules:
  0.0 306.6 jit_solution(2450881433719548013)
XLA Ops:
  0.6 0.0 copy-start.3
  0.6 5.2 %collective-permute-start.1 = (f32[8,128,128]{2,1,0:T(8,128)}, f32[8,128,128]{2,1,0:T(8,128)S(1)}, u32[]{:S(2)}, u32[]{:S(2)}) collective-permute-start(f32[8,128,128]{2,1,0:T(8,128)} %param.20), channel_id=1, source_target_pairs={{0,0},{1,64},{2,128},{3,192},{4,4},{5,68},{6,132},{7,196},{8,8},{9... | collective-permute-start | bytes 1572872 | tf_op jit(solution)/shard_map/ppermute | solution.py:431
  5.8 0.9 constant_dynamic-update-slice_fusion
  6.7 0.0 copy-done.3
  6.8 0.0 copy-start.4
  6.8 0.0 copy-start.6
  6.8 0.9 copy-done.4
  7.7 0.9 copy-done.5
  8.6 0.0 copy-done.6
  8.6 2.7 collective-permute-start
  11.3 0.1 pad.3.clone
  11.4 0.1 copy.16
  11.5 0.1 reshape.9
  11.6 0.7 copy-done.8
  12.2 0.1 add_convert_fusion
  12.3 5.1 %collective-permute-start.2 = (f32[16,128]{1,0:T(8,128)S(1)}, f32[16,128]{1,0:T(8,128)S(1)}, u32[]{:S(2)}, u32[]{:S(2)}) collective-permute-start(f32[16,128]{1,0:T(8,128)S(1)} %add_convert_fusion), channel_id=1, source_target_pairs={{0,0},{1,64},{2,128},{3,192},{4,4},{5,68},{6,132},{7,196},{8,8},{9... | collective-permute-start | bytes 24584 | tf_op jit(solution)/shard_map/ppermute | solution.py:430
  17.4 55.6 %collective-permute-done.2.ints = f32[16,128]{1,0:T(8,128)S(1)} collective-permute-done((f32[16,128]{1,0:T(8,128)S(1)}, f32[16,128]{1,0:T(8,128)S(1)}, u32[]{:S(2)}, u32[]{:S(2)}) %collective-permute-start.2) | collective-permute-done | bytes 8224 | tf_op jit(solution)/shard_map/ppermute | solution.py:430
  72.9 0.0 collective-permute-done.fields
  72.9 0.0 collective-permute-done.1.inv
  73.0 214.4 %shard_map.139 = (f32[2,192,128]{2,1,0:T(8,128)S(1)}, f32[8,128]{1,0:T(8,128)S(1)}) custom-call(f32[5,192,128]{2,1,0:T(8,128)S(1)} %collective-permute-done.fields, f32[192,192]{1,0:T(8,128)S(1)} %copy-done, f32[192,192]{1,0:T(8,128)S(1)} %copy-done.1, f32[192,128]{1,0:T(8,128)S(1)} %copy-done.2, f32[8,128,128]{2,1,0:T(8,128)S(1)} %collective-permute-done.1.inv, ...), custom_call_target="tpu_custom_call" | custom-call | tf_op jit(solution)/shard_map/pallas_call | solution.py:481
  287.4 4.5 %collective-permute-start.3 = (f32[2,192,128]{2,1,0:T(8,128)S(1)}, f32[2,192,128]{2,1,0:T(8,128)S(1)}, u32[]{:S(2)}, u32[]{:S(2)}) collective-permute-start(f32[2,192,128]{2,1,0:T(8,128)S(1)} %get-tuple-element.5), channel_id=1, source_target_pairs={{0,0},{64,1},{128,2},{192,3},{4,4},{68,5},{132,6},{196,7},{8,8},{7... | collective-permute-start | bytes 589832 | tf_op jit(solution)/shard_map/ppermute | solution.py:495
  291.9 0.5 slice.11
  292.5 13.5 %collective-permute-done.3 = f32[2,192,128]{2,1,0:T(8,128)S(1)} collective-permute-done((f32[2,192,128]{2,1,0:T(8,128)S(1)}, f32[2,192,128]{2,1,0:T(8,128)S(1)}, u32[]{:S(2)}, u32[]{:S(2)}) %collective-permute-start.3) | collective-permute-done | bytes 196640 | tf_op jit(solution)/shard_map/ppermute | solution.py:495
  305.9 0.7 fusion
  (17 shorter events, 0.1 us)
Async XLA Ops:
  0.6 6.1 %copy-start.3 = (f32[192,128]{1,0:T(8,128)S(1)}, f32[192,128]{1,0:T(8,128)}, u32[]{:S(2)}) copy-start(f32[192,128]{1,0:T(8,128)} %param.13) | copy-start | bytes 294916
  0.6 72.3 %collective-permute-start.1 = (f32[8,128,128]{2,1,0:T(8,128)}, f32[8,128,128]{2,1,0:T(8,128)S(1)}, u32[]{:S(2)}, u32[]{:S(2)}) collective-permute-start(f32[8,128,128]{2,1,0:T(8,128)} %param.20), channel_id=1, source_target_pairs={{0,0},{1,64},{2,128},{3,192},{4,4},{5,68},{6,132},{7,196},{8,8},{9... | collective-permute-start | bytes 1572872 | tf_op jit(solution)/shard_map/ppermute | solution.py:431
  6.8 0.9 copy-start.4
  6.8 1.8 copy-start.6
  7.6 0.9 copy-start.5
  7.6 3.7 %copy-start.7 = (s32[1,64,16]{1,2,0:T(8,128)S(1)}, s32[1,64,16]{1,2,0:T(8,128)}, u32[]{:S(2)}) copy-start(s32[1,64,16]{1,2,0:T(8,128)} %param.21) | copy-start | bytes 12292
  7.7 65.3 %copy-start.2 = (f32[192,128]{1,0:T(8,128)S(1)}, f32[192,128]{1,0:T(8,128)}, u32[]{:S(2)}) copy-start(f32[192,128]{1,0:T(8,128)} %modes.1) | copy-start | bytes 294916
  8.5 64.4 %copy-start = (f32[192,192]{1,0:T(8,128)S(1)}, f32[192,192]{1,0:T(8,128)}, u32[]{:S(2)}) copy-start(f32[192,192]{1,0:T(8,128)} %grad.1) | copy-start | bytes 442372
  8.5 64.4 %copy-start.1 = (f32[192,192]{1,0:T(8,128)S(1)}, f32[192,192]{1,0:T(8,128)}, u32[]{:S(2)}) copy-start(f32[192,192]{1,0:T(8,128)} %trace.1) | copy-start | bytes 442372
  8.6 64.4 %collective-permute-start = (f32[5,192,128]{2,1,0:T(8,128)S(1)}, f32[5,192,128]{2,1,0:T(8,128)S(1)}, u32[]{:S(2)}, u32[]{:S(2)}) collective-permute-start(f32[5,192,128]{2,1,0:T(8,128)S(1)} %bitcast_dynamic-update-slice_fusion), channel_id=1, source_target_pairs={{0,0},{1,64},{2,128},{3,192},{4,4},{5,68},{6,132},{7,196},{8,8},{9... | collective-permute-start | bytes 1474568 | tf_op jit(solution)/shard_map/ppermute | solution.py:429
  11.5 0.7 copy-start.8
  11.5 0.7 copy-start.9
  12.3 60.6 %collective-permute-start.2 = (f32[16,128]{1,0:T(8,128)S(1)}, f32[16,128]{1,0:T(8,128)S(1)}, u32[]{:S(2)}, u32[]{:S(2)}) collective-permute-start(f32[16,128]{1,0:T(8,128)S(1)} %add_convert_fusion), channel_id=1, source_target_pairs={{0,0},{1,64},{2,128},{3,192},{4,4},{5,68},{6,132},{7,196},{8,8},{9... | collective-permute-start | bytes 24584 | tf_op jit(solution)/shard_map/ppermute | solution.py:430
  287.4 18.5 %collective-permute-start.3 = (f32[2,192,128]{2,1,0:T(8,128)S(1)}, f32[2,192,128]{2,1,0:T(8,128)S(1)}, u32[]{:S(2)}, u32[]{:S(2)}) collective-permute-start(f32[2,192,128]{2,1,0:T(8,128)S(1)} %get-tuple-element.5), channel_id=1, source_target_pairs={{0,0},{64,1},{128,2},{192,3},{4,4},{68,5},{132,6},{196,7},{8,8},{7... | collective-permute-start | bytes 589832 | tf_op jit(solution)/shard_map/ppermute | solution.py:495

commit v2 on v1

v2 whole, which is shorter than its diff:
```python
import functools
import jax
import jax.numpy as jnp
from jax import lax
from jax.experimental import pallas as pl
from jax.experimental.pallas import tpu as pltpu
from jax.sharding import PartitionSpec as P

MESH = pl.DeviceIdType.MESH
F32 = jnp.float32
BF16 = jnp.bfloat16
AXES = ("leaf", "agg", "probe")
RELAX = 0.6
CAP = 16
NT = (((1,), (1,)), ((), ()))
X = 4

PAIR = 2


def split(value):
    high = value.astype(BF16)
    return high, (value - high.astype(F32)).astype(BF16)


def dot(left, right):
    return jnp.dot(left, right, preferred_element_type=F32)


def dot_exact(left, right_pair):
    return dot(left, right_pair[0]) + dot(left, right_pair[1])


def dot_split(left, right_pair):
    left_high, left_low = split(left)
    return dot(left_high, right_pair[0]) + (
        dot(left_low, right_pair[0]) + dot(left_high, right_pair[1])
    )


def group_steps(probes):
    def hops(step):
        return -(min(step[0], probes - step[0]) + step[1] + min(step[2], X - step[2]))

    steps = [
        (y, z, x, core)
        for y in range(probes)
        for z in range(PAIR)
        for x in range(X)
        for core in range(2)
    ][1:]
    return sorted(steps, key=hops)


def kernel(
    parts,
    probes,
    probe_in,
    visc_in,
    fric_in,
    sens_in,
    misfit_in,
    grad,
    trace,
    modes,
    inv,
    ints_in,
    out,
    trace_out,
    weights_h,
    weights_l,
    modes_h,
    modes_l,
    modes_t_h,
    modes_t_l,
    inv_h,
    inv_l,
    scatter,
    scatter_two,
    gather,
    gather_two,
    adjacent,
    group_sum,
    group_spread,
    visc,
    fric,
    misfit,
    inv_diag,
    count,
    probe_sens,
    rhs,
    first_dir,
    image,
    pre,
    traces,
    home,
    moved,
    ints,
    result_out,
    result_in,
    send,
    recv,
    sums,
    sums_in,
    solved_own,
    solved,
    dots_a,
    dots_b,
    traces_all,
    send_sem,
    recv_sem,
    move_send_sem,
    move_recv_sem,
    coarse_send_sem,
    coarse_recv_sem,
    dots_send_sem,
    dots_recv_sem,
    last_send_sem,
    last_recv_sem,
):
    leaf, core, along = lax.axis_index("leaf"), lax.axis_index("agg"), lax.axis_index("probe")
    z, x = lax.div(leaf, X), lax.rem(leaf, X)
    probe, low = lax.div(z, PAIR), lax.rem(z, PAIR)
    unit = ((along * PAIR + low) * X + x) * 2 + core
    mirror_leaf = (along * PAIR + low) * X + x
    at_home = along == probe
    ndof = grad.shape[0]
    elems = visc_in.shape[1]
    slots = parts * CAP
    halves = CAP // 2
    others = parts - 1
    rest = 2 * elems - ndof

    lows = [lax.rem(low + step, PAIR) for step in range(PAIR)]
    xs = [lax.rem(x + step, X) for step in range(X)]
    cores = [core, 1 - core]
    alongs = [lax.rem(along + step, probes) for step in range(probes)]
    leaves = [[(probe * PAIR + part) * X + place for place in xs] for part in lows]
    peers = []
    for y_step, z_step, x_step, core_step in group_steps(probes):
        device = (leaves[z_step][x_step], cores[core_step], alongs[y_step])
        peer = ((alongs[y_step] * PAIR + lows[z_step]) * X + xs[x_step]) * 2 + cores[core_step]
        peers.append((device, peer))
    mates = [
        ((lax.rem(probe + step, probes) * PAIR + low) * X + x, core, along)
        for step in range(1, probes)
    ]
    mirrors = [(mirror_leaf, side, probe) for side in cores]

    barrier = pltpu.get_barrier_semaphore()
    for device in [device for device, _ in peers] + mates:
        pl.semaphore_signal(barrier, inc=1, device_id=device, device_id_type=MESH)

    @pl.when(jnp.logical_not(at_home))
    def _():
        for device in mirrors:
            pl.semaphore_signal(barrier, inc=1, device_id=device, device_id_type=MESH)

    def wait_bytes(ref, sem):
        pltpu.make_async_copy(ref, ref, sem).wait()

    def mirror_start(source, target, send_at, recv_at, step=0):
        def remote():
            return pltpu.make_async_remote_copy(
                src_ref=source,
                dst_ref=target,
                send_sem=send_at,
                recv_sem=recv_at,
                device_id=mirrors[step],
                device_id_type=MESH,
            )

        if step:
            remote().start()
        else:

            @pl.when(at_home)
            def _():
                pltpu.make_async_copy(source, target, recv_at).start()

            @pl.when(jnp.logical_not(at_home))
            def _():
                remote().start()

    def mirror_sent(source, send_at, step=0):
        if step:
            wait_bytes(source, send_at)
        else:

            @pl.when(jnp.logical_not(at_home))
            def _():
                wait_bytes(source, send_at)

    rows = lax.broadcasted_iota(jnp.int32, (elems, elems), 0).astype(F32)

    def one_hot(ref, row):
        return (ref[pl.ds(row, 1), :] == rows).astype(F32)

    base = slots // elems

    def adjacency(ref):
        ends = [one_hot(ref, base + end).astype(BF16) for end in range(2)]
        near = lax.dot_general(ends[0], ends[1], NT, preferred_element_type=F32)
        return near + lax.dot_general(ends[1], ends[0], NT, preferred_element_type=F32)

    home[0] = sens_in[...] * probe_in[0]
    touching = jnp.sum(adjacency(ints_in), axis=0, keepdims=True)
    for block in range(base):
        touching = touching + jnp.sum(one_hot(ints_in, block).T, axis=0, keepdims=True)
    grad_t, trace_t = grad[...].T, trace[...].T
    trace_square = jnp.sum(trace_t * trace_t, axis=1, keepdims=True)
    diag = dot_split(grad_t * grad_t, split(visc_in[...])) + fric_in[...]
    home[1] = RELAX / (diag + trace_square * touching)
    for turn in range(2):
        recv[turn, unit] = jnp.zeros(recv.shape[2:], F32)

    @pl.when(at_home)
    def _():
        pl.semaphore_wait(barrier, others + probes - 1)

    @pl.when(jnp.logical_not(at_home))
    def _():
        pl.semaphore_wait(barrier, others + probes + 1)

    sources = [ints_in, home.at[0], home.at[1], visc_in, fric_in, misfit_in]
    targets = [ints] + [moved.at[which] for which in range(5)]
    for which, (source, target) in enumerate(zip(sources, targets)):
        mirror_start(source, target, move_send_sem.at[which], move_recv_sem.at[which])

    def moved_end(which):
        wait_bytes(targets[which], move_recv_sem.at[which])
        mirror_sent(sources[which], move_send_sem.at[which])

    for slot, matrix in enumerate((grad_t, grad[...], trace_t, trace[...])):
        weights_h[slot], weights_l[slot] = split(matrix)
    modes_h[...], modes_l[...] = split(modes[...])
    modes_t_h[...], modes_t_l[...] = split(modes[...].T)
    for block in range(inv.shape[0]):
        inv_h[block], inv_l[block] = split(inv[block])
    moved_end(0)
    cross = jnp.zeros((elems, 1), F32)
    for block in range(base):
        hot = one_hot(ints, block)
        cross = cross + jnp.sum(hot, axis=1, keepdims=True)
        here = pl.ds(block * elems, elems)
        scatter[:, here] = hot.astype(BF16)
        hot_t = hot.T
        gather[here, :] = hot_t.astype(BF16)
        paired = hot_t.reshape(elems // CAP, 2, halves, elems)
        half = pl.ds(block * (elems // 2), elems // 2)
        gather_two[half, :elems] = paired[:, 0].reshape(elems // 2, elems).astype(BF16)
        gather_two[half, elems:] = paired[:, 1].reshape(elems // 2, elems).astype(BF16)
    for block in range(base // 2):
        here = pl.ds(block * elems, elems)
        scatter_two[:elems, here] = gather_two[here, :elems].astype(F32).T.astype(BF16)
        scatter_two[elems:, here] = gather_two[here, elems:].astype(F32).T.astype(BF16)
    near_pairs = adjacency(ints)
    adjacent[...] = near_pairs.astype(BF16)
    count[...] = cross + jnp.sum(near_pairs, axis=1, keepdims=True)
    hot = one_hot(ints, base + 2)
    group_sum[...] = hot[: sums.shape[0]].astype(BF16)
    group_spread[...] = hot.T.astype(BF16)
    moved_end(1)
    start = moved[0].T
    probe_sens[...] = start
    rhs[...] = start
    solved[...] = jnp.zeros_like(solved)
    moved_end(2)
    inv_diag[...] = moved[1].T

    def weight(slot):
        return weights_h[slot], weights_l[slot]

    def wait_blocks(turn, sem):
        wait_bytes(recv.at[turn, pl.ds(0, others)], sem.at[turn])

    def operate(value, turn, started=None):
        traced = dot_split(value, weight(2))
        high, low_part = split(traced)
        blank = jnp.zeros((elems, rest), BF16)
        send[turn, :, :CAP, :] = dot_exact(
            gather[...], (high[:, :elems], low_part[:, :elems])
        ).reshape(parts, CAP, elems)

        def two(piece):
            tail = piece[:, elems:]
            return jnp.concatenate(
                [jnp.concatenate([tail, blank], 1), jnp.concatenate([blank, tail], 1)], 0
            )

        send[turn, :, CAP:, :] = dot_exact(
            gather_two[...], (two(high), two(low_part))
        ).reshape(parts, halves, elems)
        for device, peer in peers:
            pltpu.make_async_remote_copy(
                src_ref=send.at[turn, peer],
                dst_ref=recv.at[turn, unit],
                send_sem=send_sem.at[turn],
                recv_sem=recv_sem.at[turn],
                device_id=device,
                device_id_type=MESH,
            ).start()
        if started is not None:
            started()
        inner = dot_split(visc[...] * dot_split(value, weight(0)), weight(1))
        near = count[...] * traced - dot_exact(adjacent[...], (high, low_part))
        inner = inner + fric[...] * value
        wait_blocks(turn, recv_sem)
        first = dot_exact(scatter[...], split(recv[turn, :, :CAP, :].reshape(slots, elems)))
        second = dot_exact(
            scatter_two[...], split(recv[turn, :, CAP:, :].reshape(slots // 2, elems))
        )
        second = second[:elems, :rest] + second[elems:, rest:]
        near = near - jnp.concatenate([first, second], 1)
        result = inner + dot_split(near, weight(3))
        wait_blocks(turn, send_sem)
        return result

    own_aggs = inv.shape[0]

    def agg_rows(side):
        return pl.ds(pl.multiple_of(side * own_aggs, own_aggs), own_aggs)

    def coarse_start(residual):
        projected = dot_split(residual, (modes_h[...], modes_l[...]))
        sums[...] = dot_exact(group_sum[...], split(projected))
        for step, side in enumerate(cores):
            mirror_start(
                sums.at[agg_rows(side)],
                sums_in.at[step],
                coarse_send_sem.at[step],
                coarse_recv_sem.at[step],
                step,
            )

    def coarse_solve():
        for step, side in enumerate(cores):
            wait_bytes(sums_in.at[step], coarse_recv_sem.at[step])
            mirror_sent(sums.at[agg_rows(side)], coarse_send_sem.at[step], step)
        total = sums_in[0] + sums_in[1]
        row = lax.broadcasted_iota(jnp.int32, total.shape, 0)
        result = jnp.zeros_like(total)
        for block in range(own_aggs):
            one = dot_split(total, (inv_h[block], inv_l[block]))
            result = jnp.where(row == block, one, result)
        solved_own[...] = result
        for step in range(2):
            mirror_start(
                solved_own,
                solved.at[agg_rows(core)],
                coarse_send_sem.at[2 + step],
                coarse_recv_sem.at[2 + step],
                step,
            )

    def coarse_end():
        for step, side in enumerate(cores):
            wait_bytes(solved.at[agg_rows(side)], coarse_recv_sem.at[2 + step])
            mirror_sent(solved_own, coarse_send_sem.at[2 + step], step)
        spread = dot_exact(group_spread[...], split(solved[...]))
        return dot_split(spread, (modes_t_h[...], modes_t_l[...]))

    def precondition(residual_ref, turn, started=None):
        pre[...] = residual_ref[...] * inv_diag[...]
        coarse_start(residual_ref[...])
        pre[...] += (residual_ref[...] - operate(pre[...], turn, started)) * inv_diag[...]
        coarse_solve()
        pre[...] += (residual_ref[...] - operate(pre[...], 1 - turn)) * inv_diag[...]
        return pre[...] + coarse_end()

    def lanes(left, right):
        total = jnp.sum(left * right, axis=0, keepdims=True)
        tail = jnp.concatenate([total[:, elems:], jnp.zeros((1, rest), F32)], 1)
        return total[:, :elems] + tail

    def dots_start(buffer, which, pieces):
        column = jnp.concatenate(list(pieces) + [jnp.zeros((8 - len(pieces), elems), F32)], 0)
        column = jnp.sum(column, axis=1, keepdims=True)
        across = lax.broadcasted_iota(jnp.int32, (8, elems), 1)
        down = lax.broadcasted_iota(jnp.int32, (8, elems), 0)
        buffer[unit] = jnp.sum(jnp.where(across == down, column, 0.0), axis=0, keepdims=True)
        for device, _ in peers:
            pltpu.make_async_remote_copy(
                src_ref=buffer.at[unit],
                dst_ref=buffer.at[unit],
                send_sem=dots_send_sem.at[which],
                recv_sem=dots_recv_sem.at[which],
                device_id=device,
                device_id_type=MESH,
            ).start()

    def dots_end(buffer, which):
        blocks = buffer.at[pl.ds(0, others)]
        wait_bytes(blocks, dots_recv_sem.at[which])
        wait_bytes(blocks, dots_send_sem.at[which])
        total = jnp.sum(buffer[...], axis=0)
        return [total[:, lane : lane + 1] for lane in range(8)]

    @pl.loop(0, 2)
    def _(solve):
        def first_time():
            @pl.when(solve == 0)
            def _():
                moved_end(3)
                visc[...] = moved[2].T
                moved_end(4)
                fric[...] = moved[3].T

        first_dir[...] = precondition(rhs, 0, first_time)
        image[...] = operate(first_dir[...], 0)
        dots_start(
            dots_a,
            0,
            [lanes(rhs[...], first_dir[...]), lanes(first_dir[...], image[...])],
        )
        second = precondition(image, 1)
        energy, curve, *_ = dots_end(dots_a, 0)
        step = energy / curve
        second = first_dir[...] - step * second
        residual = rhs[...] - step * image[...]
        pre[...] = second
        second_image = operate(pre[...], 1)
        second = pre[...]
        dots_start(
            dots_b,
            1,
            [
                lanes(residual, second),
                lanes(second, second_image),
                lanes(second, image[...]),
                lanes(probe_sens[...], first_dir[...]),
                lanes(probe_sens[...], second),
            ],
        )

        @pl.when(solve == 0)
        def _():
            moved_end(5)
            misfit[...] = moved[4].T

        energy_next, curve_zz, curve_zp, trace_first, trace_second, *_ = dots_end(dots_b, 1)
        ratio = energy_next / energy
        curve_next = curve_zz + 2.0 * ratio * curve_zp + ratio * ratio * curve
        step_next = energy_next / curve_next
        weight_first = step + step_next * ratio
        result = weight_first * first_dir[...] + step_next * pre[...]
        result_out[solve] = result.T
        mirror_start(
            result_out.at[solve],
            result_in.at[solve],
            move_send_sem.at[6 + solve],
            move_recv_sem.at[6 + solve],
        )
        rhs[...] = misfit[...] * result
        value = weight_first * trace_first + step_next * trace_second
        traces[...] = jnp.broadcast_to(value, traces.shape)

    traces_all[probe] = traces[...]
    for device in mates:
        pltpu.make_async_remote_copy(
            src_ref=traces,
            dst_ref=traces_all.at[probe],
            send_sem=last_send_sem,
            recv_sem=last_recv_sem,
            device_id=device,
            device_id_type=MESH,
        ).start()
    for solve in range(2):
        wait_bytes(result_in.at[solve], move_recv_sem.at[6 + solve])
        mirror_sent(result_out.at[solve], move_send_sem.at[6 + solve])
    out[0] = result_in[0]
    out[1] = result_in[1] * sens_in[...]
    blocks = traces_all.at[pl.ds(0, probes - 1)]
    wait_bytes(blocks, last_recv_sem)
    wait_bytes(blocks, last_send_sem)
    trace_out[...] = jnp.sum(traces_all[...], axis=0) / probes


def on_device(
    probes,
    viscosity,
    friction,
    sensitivity,
    misfit_weight,
    grad_ref,
    trace_ref,
    coarse_modes,
    coarse_inv,
    peer_slots,
    local_pairs,
    elem_agg,
):
    leaves, aggs, count = (lax.axis_size(axis) for axis in AXES)
    parts = leaves * aggs
    ndof, elems = viscosity.shape
    own_aggs, modes_n = coarse_inv.shape[:2]
    slots = parts * CAP
    ints = jnp.concatenate(
        [
            peer_slots.reshape(slots // elems, elems),
            local_pairs,
            elem_agg[None],
            jnp.zeros((5, elems), jnp.int32),
        ]
    ).astype(F32)

    def vmem(*shape, dtype=F32):
        return pltpu.VMEM(shape, dtype)

    field = vmem(elems, ndof)
    block_rows = CAP + CAP // 2
    dma = pltpu.SemaphoreType.DMA
    scratch = [
        vmem(4, ndof, ndof, dtype=BF16),
        vmem(4, ndof, ndof, dtype=BF16),
        vmem(ndof, modes_n, dtype=BF16),
        vmem(ndof, modes_n, dtype=BF16),
        vmem(modes_n, ndof, dtype=BF16),
        vmem(modes_n, ndof, dtype=BF16),
        vmem(own_aggs, modes_n, modes_n, dtype=BF16),
        vmem(own_aggs, modes_n, modes_n, dtype=BF16),
        vmem(elems, slots, dtype=BF16),
        vmem(2 * elems, slots // 2, dtype=BF16),
        vmem(slots, elems, dtype=BF16),
        vmem(slots // 2, 2 * elems, dtype=BF16),
        vmem(elems, elems, dtype=BF16),
        vmem(aggs * own_aggs, elems, dtype=BF16),
        vmem(elems, elems, dtype=BF16),
        field,
        field,
        field,
        field,
        vmem(elems, 1),
        field,
        field,
        field,
        field,
        field,
        vmem(8, elems),
        vmem(2, ndof, elems),
        vmem(5, ndof, elems),
        vmem(*ints.shape),
        vmem(2, ndof, elems),
        vmem(2, ndof, elems),
        vmem(2, parts, block_rows, elems),
        vmem(2, parts, block_rows, elems),
        vmem(aggs * own_aggs, modes_n),
        vmem(2, own_aggs, modes_n),
        vmem(own_aggs, modes_n),
        vmem(elems, modes_n),
        vmem(parts, 1, elems),
        vmem(parts, 1, elems),
        vmem(count, 8, elems),
        dma((2,)),
        dma((2,)),
        dma((8,)),
        dma((8,)),
        dma((4,)),
        dma((4,)),
        dma((2,)),
        dma((2,)),
        dma,
        dma,
    ]
    out, trace_tile = pl.pallas_call(
        functools.partial(kernel, parts, count),
        out_shape=(
            jax.ShapeDtypeStruct((2, ndof, elems), F32),
            jax.ShapeDtypeStruct((8, elems), F32),
        ),
        in_specs=[pl.BlockSpec(memory_space=pltpu.VMEM)] * 10,
        out_specs=(pl.BlockSpec(memory_space=pltpu.VMEM),) * 2,
        scratch_shapes=scratch,
        compiler_params=pltpu.CompilerParams(
            collective_id=0, has_side_effects=True, vmem_limit_bytes=48 * 1024 * 1024
        ),
    )(
        probes,
        viscosity,
        friction,
        sensitivity,
        misfit_weight,
        grad_ref,
        trace_ref,
        coarse_modes,
        coarse_inv,
        ints,
    )
    return out[0][None], out[1][None], trace_tile[0, 0]


def solution(mesh):
    in_specs = (
        P("probe", None, ("leaf", "agg")),
        P(None, ("leaf", "agg")),
        P(None, ("leaf", "agg")),
        P(None, ("leaf", "agg")),
        P(None, ("leaf", "agg")),
        P(),
        P(),
        P(),
        P(("leaf", "agg"), None, None),
        P(("leaf", "agg"), None, None),
        P(None, ("leaf", "agg")),
        P(("leaf", "agg")),
    )
    out_specs = (P("probe", None, ("leaf", "agg")), P("probe", None, ("leaf", "agg")), P())
    return jax.shard_map(
        on_device, mesh=mesh, in_specs=in_specs, out_specs=out_specs, check_vma=False
    )
```

time: 307 us -> 236 us (0.77)
  waiting for transfers between devices: 69 us -> 0 us
  starting transfers between devices: 17.5 us -> 0 us
  Pallas kernels: 214 us -> 223 us
  local copies, waits for them, and re-layouts: 4.81 us -> 11 us
    ppermute x4 -> x0, waiting for transfers between devices: 69 us -> none  [the longest x1 55.6 us: on_device(): ints = lax.ppermute(ints, AXES, moves)]
    ppermute x4 -> x0, starting transfers between devices: 17.5 us -> none  [the longest x1 5.2 us: on_device(): coarse_inv = lax.ppermute(coarse_inv, AXES, moves)]
    pallas_call x1, Pallas kernels: 214 us -> 223 us  [on_device(): pl.pallas_call(functools.partial(kernel, parts, count), out_shape=(jax.Sh...]
    unnamed x25 -> x23, local copies, waits for them, and re-layouts: 3.45 us -> 9.62 us
  transfers between devices with their start and end apart: 4 -> 0, of which waited for: 2 -> 0; matrix products, arithmetic and copies ran while one was open for 1% -> 0% of each run, Pallas kernels for 0% -> 0%
where the time goes in v2:
time: 236 us; the launch traced here: 234 us
  Pallas kernels  223 us (94%)
  local copies, waits for them, and re-layouts  11 us (5%)
    pallas_call x1, Pallas kernels, on_device(): pl.pallas_call(functools.partial(kernel, parts, count), out_shape=(jax.Sh...  223 us
    unnamed x23, local copies, waits for them, and re-layouts  9.62 us

profile of v2, /device:TPU:8, one launch (start us, length us, event | category | flops | bytes accessed | tf_op | source)
XLA Modules:
  0.0 234.3 jit_solution(17401744212298164472)
XLA Ops:
  0.6 0.1 pad.3.clone
  0.7 0.8 copy.16
  1.5 0.0 copy-start.9
  1.5 0.0 copy-start.10
  1.5 0.1 reshape.9
  1.6 0.6 copy-done.9
  2.2 0.0 copy-done.10
  2.2 0.1 add_convert_fusion.ints_in
  2.3 0.0 copy-start
  2.3 1.0 copy-done
  3.3 0.0 copy-start.1
  3.3 0.9 copy-done.1
  4.2 0.0 copy-start.2
  4.2 0.9 copy-done.2
  5.1 0.0 copy-start.3
  5.2 0.9 copy-done.3
  6.0 0.9 copy-done.4
  6.9 0.9 copy-done.5
  7.8 0.9 copy-done.6
  8.7 0.9 copy-done.7
  9.6 0.9 copy-done.8
  10.5 222.6 %shard_map.139 = (f32[2,192,128]{2,1,0:T(8,128)S(1)}, f32[8,128]{1,0:T(8,128)S(1)}) custom-call(f32[1,192,128]{2,1,0:T(8,128)S(1)} %copy-done.3, f32[192,128]{1,0:T(8,128)S(1)} %copy-done.4, f32[192,128]{1,0:T(8,128)S(1)} %copy-done.5, f32[192,128]{1,0:T(8,128)S(1)} %copy-done.6, f32[192,128]{1,0:T(8,128)S(1)} %copy-done.7, f32[192,192]{1,0:T(8,128)S(1)} %copy-done.1, ...), custom_call_target="tpu_custom_call" | custom-call | tf_op jit(solution)/shard_map/pallas_call | solution.py:565
  233.1 0.5 slice.11
  233.6 0.7 fusion
  (6 shorter events, 0.0 us)
Async XLA Ops:
  1.5 0.7 copy-start.9
  1.5 0.7 copy-start.10
  2.3 1.0 copy-start
  3.3 0.9 copy-start.1
  4.2 0.9 copy-start.2
  5.1 0.9 copy-start.3
  6.0 0.9 copy-start.4
  6.9 0.9 copy-start.5
  7.8 0.9 copy-start.6
  8.7 0.9 copy-start.7
  9.6 0.9 copy-start.8

commit v3 on v2

--- a/solution.py
+++ b/solution.py
@@ -55,18 +55,26 @@
 def kernel(
     parts,
     probes,
+    probe_far,
+    visc_far,
+    fric_far,
+    sens_far,
+    misfit_far,
+    grad_far,
+    trace_far,
+    modes_far,
+    inv_far,
+    ints_in,
+    out,
+    trace_out,
     probe_in,
     visc_in,
     fric_in,
     sens_in,
-    misfit_in,
     grad,
     trace,
     modes,
     inv,
-    ints_in,
-    out,
-    trace_out,
     weights_h,
     weights_l,
     modes_h,
@@ -87,6 +95,7 @@
     misfit,
     inv_diag,
     count,
+    count_near,
     probe_sens,
     rhs,
     first_dir,
@@ -117,7 +126,25 @@
     dots_recv_sem,
     last_send_sem,
     last_recv_sem,
+    load_sem,
 ):
+    loads = [
+        pltpu.make_async_copy(far, near, load_sem.at[which])
+        for which, (far, near) in enumerate(
+            [
+                (visc_far, visc_in),
+                (grad_far, grad),
+                (fric_far, fric_in),
+                (trace_far, trace),
+                (sens_far, sens_in),
+                (probe_far, probe_in),
+                (modes_far, modes),
+                (inv_far, inv),
+            ]
+        )
+    ]
+    for load in loads:
+        load.start()
     leaf, core, along = lax.axis_index("leaf"), lax.axis_index("agg"), lax.axis_index("probe")
     z, x = lax.div(leaf, X), lax.rem(leaf, X)
     probe, low = lax.div(z, PAIR), lax.rem(z, PAIR)
@@ -136,11 +163,24 @@
     cores = [core, 1 - core]
     alongs = [lax.rem(along + step, probes) for step in range(probes)]
     leaves = [[(probe * PAIR + part) * X + place for place in xs] for part in lows]
-    peers = []
-    for y_step, z_step, x_step, core_step in group_steps(probes):
+
+    def reached(step):
+        y_step, z_step, x_step, core_step = step
         device = (leaves[z_step][x_step], cores[core_step], alongs[y_step])
         peer = ((alongs[y_step] * PAIR + lows[z_step]) * X + xs[x_step]) * 2 + cores[core_step]
-        peers.append((device, peer))
+        return device, peer
+
+    steps = group_steps(probes)
+    peers = [reached(step) for step in steps]
+    inverse = {
+        step: ((probes - step[0]) % probes, step[1], (X - step[2]) % X, step[3]) for step in steps
+    }
+    pair_steps = [
+        step
+        for step in steps
+        if step == inverse[step]
+        or (step < inverse[step]) == ((step[1] + step[3]) % 2 == 0)
+    ]
     mates = [
         ((lax.rem(probe + step, probes) * PAIR + low) * X + x, core, along)
         for step in range(1, probes)
@@ -203,14 +243,19 @@
         near = lax.dot_general(ends[0], ends[1], NT, preferred_element_type=F32)
         return near + lax.dot_general(ends[1], ends[0], NT, preferred_element_type=F32)
 
-    home[0] = sens_in[...] * probe_in[0]
-    touching = jnp.sum(adjacency(ints_in), axis=0, keepdims=True)
+    def inverse_diagonal(visc_t, fric_t, counts):
+        square = grad[...] * grad[...]
+        trace_square = jnp.sum(trace[...] * trace[...], axis=0, keepdims=True)
+        return RELAX / (dot_split(visc_t, split(square)) + fric_t + counts * trace_square)
+
+    touching = jnp.zeros((elems, 1), F32)
     for block in range(base):
-        touching = touching + jnp.sum(one_hot(ints_in, block).T, axis=0, keepdims=True)
-    grad_t, trace_t = grad[...].T, trace[...].T
-    trace_square = jnp.sum(trace_t * trace_t, axis=1, keepdims=True)
-    diag = dot_split(grad_t * grad_t, split(visc_in[...])) + fric_in[...]
-    home[1] = RELAX / (diag + trace_square * touching)
+        touching = touching + jnp.sum(one_hot(ints_in, block), axis=1, keepdims=True)
+    touching = touching + jnp.sum(adjacency(ints_in), axis=1, keepdims=True)
+    for load in loads[:6]:
+        load.wait()
+    home_diag = inverse_diagonal(visc_in[...].T, fric_in[...].T, touching)
+    home[...] = ((sens_in[...] * probe_in[0]).T * home_diag).T
     for turn in range(2):
         recv[turn, unit] = jnp.zeros(recv.shape[2:], F32)
 
@@ -222,17 +267,25 @@
     def _():
         pl.semaphore_wait(barrier, others + probes + 1)
 
-    sources = [ints_in, home.at[0], home.at[1], visc_in, fric_in, misfit_in]
-    targets = [ints] + [moved.at[which] for which in range(5)]
-    for which, (source, target) in enumerate(zip(sources, targets)):
-        mirror_start(source, target, move_send_sem.at[which], move_recv_sem.at[which])
+    sources = [ints_in, home, visc_in, fric_in, misfit_far]
+    targets = [ints] + [moved.at[which] for which in range(4)]
+
+    def moved_start(which):
+        mirror_start(
+            sources[which], targets[which], move_send_sem.at[which], move_recv_sem.at[which]
+        )
+
+    for which in range(4):
+        moved_start(which)
 
     def moved_end(which):
         wait_bytes(targets[which], move_recv_sem.at[which])
         mirror_sent(sources[which], move_send_sem.at[which])
 
-    for slot, matrix in enumerate((grad_t, grad[...], trace_t, trace[...])):
+    for slot, matrix in enumerate((grad[...].T, grad[...], trace[...].T, trace[...])):
         weights_h[slot], weights_l[slot] = split(matrix)
+    for load in loads[6:]:
+        load.wait()
     modes_h[...], modes_l[...] = split(modes[...])
     modes_t_h[...], modes_t_l[...] = split(modes[...].T)
     for block in range(inv.shape[0]):
@@ -256,25 +309,22 @@
         scatter_two[elems:, here] = gather_two[here, elems:].astype(F32).T.astype(BF16)
     near_pairs = adjacency(ints)
     adjacent[...] = near_pairs.astype(BF16)
-    count[...] = cross + jnp.sum(near_pairs, axis=1, keepdims=True)
+    count_near[...] = jnp.sum(near_pairs, axis=1, keepdims=True)
+    count[...] = cross + count_near[...]
     hot = one_hot(ints, base + 2)
     group_sum[...] = hot[: sums.shape[0]].astype(BF16)
     group_spread[...] = hot.T.astype(BF16)
+    solved[...] = jnp.zeros_like(solved)
     moved_end(1)
-    start = moved[0].T
-    probe_sens[...] = start
-    rhs[...] = start
-    solved[...] = jnp.zeros_like(solved)
-    moved_end(2)
-    inv_diag[...] = moved[1].T
+    pre[...] = moved[0].T
 
     def weight(slot):
         return weights_h[slot], weights_l[slot]
 
-    def wait_blocks(turn, sem):
-        wait_bytes(recv.at[turn, pl.ds(0, others)], sem.at[turn])
-
-    def operate(value, turn, started=None):
+    def wait_blocks(turn, sem, blocks=others):
+        wait_bytes(recv.at[turn, pl.ds(0, blocks)], sem.at[turn])
+
+    def send_traces(value, turn, receivers):
         traced = dot_split(value, weight(2))
         high, low_part = split(traced)
         blank = jnp.zeros((elems, rest), BF16)
@@ -291,7 +341,7 @@
         send[turn, :, CAP:, :] = dot_exact(
             gather_two[...], (two(high), two(low_part))
         ).reshape(parts, halves, elems)
-        for device, peer in peers:
+        for device, peer in receivers:
             pltpu.make_async_remote_copy(
                 src_ref=send.at[turn, peer],
                 dst_ref=recv.at[turn, unit],
@@ -300,6 +350,29 @@
                 device_id=device,
                 device_id_type=MESH,
             ).start()
+        return traced, high, low_part
+
+    def energy(value, turn):
+        traced, high, low_part = send_traces(value, turn, [reached(step) for step in pair_steps])
+        strain = dot_split(value, weight(0))
+        near = count_near[...] * traced - dot_exact(adjacent[...], (high, low_part))
+        total = lanes(visc[...] * strain, strain)
+        total = total + lanes(fric[...] * value, value) + lanes(near, traced)
+        wait_blocks(turn, recv_sem, len(pair_steps))
+        once = jnp.zeros(recv.shape[2:], F32)
+        twice = jnp.zeros(recv.shape[2:], F32)
+        for step in pair_steps:
+            _, peer = reached(inverse[step])
+            jump = send[turn, peer] - recv[turn, peer]
+            if step == inverse[step]:
+                twice = twice + jump * jump
+            else:
+                once = once + jump * jump
+        wait_blocks(turn, send_sem, len(pair_steps))
+        return total + jnp.sum(once + 0.5 * twice, axis=0, keepdims=True)
+
+    def operate(value, turn, started=None):
+        traced, high, low_part = send_traces(value, turn, peers)
         if started is not None:
             started()
         inner = dot_split(visc[...] * dot_split(value, weight(0)), weight(1))
@@ -360,12 +433,16 @@
         spread = dot_exact(group_spread[...], split(solved[...]))
         return dot_split(spread, (modes_t_h[...], modes_t_l[...]))
 
-    def precondition(residual_ref, turn, started=None):
-        pre[...] = residual_ref[...] * inv_diag[...]
-        coarse_start(residual_ref[...])
-        pre[...] += (residual_ref[...] - operate(pre[...], turn, started)) * inv_diag[...]
+    def precondition(residual_ref, turn, started, later=None):
+        def beside():
+            started()
+            coarse_start(residual_ref[...])
+
+        changed = operate(pre[...], turn, beside)
+        pre[...] += (residual_ref[...] - changed) * inv_diag[...]
         coarse_solve()
-        pre[...] += (residual_ref[...] - operate(pre[...], 1 - turn)) * inv_diag[...]
+        changed = operate(pre[...], 1 - turn, later)
+        pre[...] += (residual_ref[...] - changed) * inv_diag[...]
         return pre[...] + coarse_end()
 
     def lanes(left, right):
@@ -373,27 +450,45 @@
         tail = jnp.concatenate([total[:, elems:], jnp.zeros((1, rest), F32)], 1)
         return total[:, :elems] + tail
 
-    def dots_start(buffer, which, pieces):
+    stage_steps = [
+        [step for step in steps if step[2:] == (0, 0)],
+        [step for step in steps if step[:2] == (0, 0)],
+    ]
+    stage_spots = [along * PAIR + low, x * 2 + core]
+    stage_buffers = [dots_a, dots_b]
+
+    def dots_send(which, stage, row):
+        spot = stage_buffers[stage].at[which, stage_spots[stage]]
+        spot[...] = row
+        for step in stage_steps[stage]:
+            pltpu.make_async_remote_copy(
+                src_ref=spot,
+                dst_ref=spot,
+                send_sem=dots_send_sem.at[which, stage],
+                recv_sem=dots_recv_sem.at[which, stage],
+                device_id=reached(step)[0],
+                device_id_type=MESH,
+            ).start()
+
+    def dots_sum(which, stage):
+        blocks = stage_buffers[stage].at[which, pl.ds(0, len(stage_steps[stage]))]
+        wait_bytes(blocks, dots_recv_sem.at[which, stage])
+        wait_bytes(blocks, dots_send_sem.at[which, stage])
+        return jnp.sum(stage_buffers[stage][which], axis=0)
+
+    def dots_start(which, pieces):
         column = jnp.concatenate(list(pieces) + [jnp.zeros((8 - len(pieces), elems), F32)], 0)
         column = jnp.sum(column, axis=1, keepdims=True)
         across = lax.broadcasted_iota(jnp.int32, (8, elems), 1)
         down = lax.broadcasted_iota(jnp.int32, (8, elems), 0)
-        buffer[unit] = jnp.sum(jnp.where(across == down, column, 0.0), axis=0, keepdims=True)
-        for device, _ in peers:
-            pltpu.make_async_remote_copy(
-                src_ref=buffer.at[unit],
-                dst_ref=buffer.at[unit],
-                send_sem=dots_send_sem.at[which],
-                recv_sem=dots_recv_sem.at[which],
-                device_id=device,
-                device_id_type=MESH,
-            ).start()
-
-    def dots_end(buffer, which):
-        blocks = buffer.at[pl.ds(0, others)]
-        wait_bytes(blocks, dots_recv_sem.at[which])
-        wait_bytes(blocks, dots_send_sem.at[which])
-        total = jnp.sum(buffer[...], axis=0)
+        row = jnp.sum(jnp.where(across == down, column, 0.0), axis=0, keepdims=True)
+        dots_send(which, 0, row)
+
+    def dots_next(which):
+        dots_send(which, 1, dots_sum(which, 0))
+
+    def dots_end(which):
+        total = dots_sum(which, 1)
         return [total[:, lane : lane + 1] for lane in range(8)]
 
     @pl.loop(0, 2)
@@ -401,32 +496,38 @@
         def first_time():
             @pl.when(solve == 0)
             def _():
+                moved_end(2)
+                visc[...] = moved[1].T
                 moved_end(3)
-                visc[...] = moved[2].T
-                moved_end(4)
-                fric[...] = moved[3].T
+                fric[...] = moved[2].T
+                inv_diag[...] = inverse_diagonal(visc[...], fric[...], count[...])
+                start = pre[...] / inv_diag[...]
+                probe_sens[...] = start
+                rhs[...] = start
+                moved_start(4)
 
         first_dir[...] = precondition(rhs, 0, first_time)
         image[...] = operate(first_dir[...], 0)
-        dots_start(
-            dots_a,
-            0,
-            [lanes(rhs[...], first_dir[...]), lanes(first_dir[...], image[...])],
-        )
-        second = precondition(image, 1)
-        energy, curve, *_ = dots_end(dots_a, 0)
-        step = energy / curve
+        pre[...] = image[...] * inv_diag[...]
+
+        def sums_first():
+            dots_start(
+                0, [lanes(rhs[...], first_dir[...]), lanes(first_dir[...], image[...])]
+            )
+
+        second = precondition(image, 1, sums_first, functools.partial(dots_next, 0))
+        energy_now, curve, *_ = dots_end(0)
+        step = energy_now / curve
         second = first_dir[...] - step * second
         residual = rhs[...] - step * image[...]
         pre[...] = second
-        second_image = operate(pre[...], 1)
+        energy_second = energy(pre[...], 1)
         second = pre[...]
         dots_start(
-            dots_b,
             1,
             [
                 lanes(residual, second),
-                lanes(second, second_image),
+                energy_second,
                 lanes(second, image[...]),
                 lanes(probe_sens[...], first_dir[...]),
                 lanes(probe_sens[...], second),
@@ -435,11 +536,12 @@
 
         @pl.when(solve == 0)
         def _():
-            moved_end(5)
-            misfit[...] = moved[4].T
-
-        energy_next, curve_zz, curve_zp, trace_first, trace_second, *_ = dots_end(dots_b, 1)
-        ratio = energy_next / energy
+            moved_end(4)
+            misfit[...] = moved[3].T
+
+        dots_next(1)
+        energy_next, curve_zz, curve_zp, trace_first, trace_second, *_ = dots_end(1)
+        ratio = energy_next / energy_now
         curve_next = curve_zz + 2.0 * ratio * curve_zp + ratio * ratio * curve
         step_next = energy_next / curve_next
         weight_first = step + step_next * ratio
@@ -451,7 +553,9 @@
             move_send_sem.at[6 + solve],
             move_recv_sem.at[6 + solve],
         )
-        rhs[...] = misfit[...] * result
+        source = misfit[...] * result
+        rhs[...] = source
+        pre[...] = source * inv_diag[...]
         value = weight_first * trace_first + step_next * trace_second
         traces[...] = jnp.broadcast_to(value, traces.shape)
 
@@ -511,6 +615,14 @@
     block_rows = CAP + CAP // 2
     dma = pltpu.SemaphoreType.DMA
     scratch = [
+        vmem(1, ndof, elems),
+        vmem(ndof, elems),
+        vmem(ndof, elems),
+        vmem(ndof, elems),
+        vmem(ndof, ndof),
+        vmem(ndof, ndof),
+        vmem(ndof, modes_n),
+        vmem(own_aggs, modes_n, modes_n),
         vmem(4, ndof, ndof, dtype=BF16),
         vmem(4, ndof, ndof, dtype=BF16),
         vmem(ndof, modes_n, dtype=BF16),
@@ -531,14 +643,15 @@
         field,
         field,
         vmem(elems, 1),
+        vmem(elems, 1),
         field,
         field,
         field,
         field,
         field,
         vmem(8, elems),
-        vmem(2, ndof, elems),
-        vmem(5, ndof, elems),
+        vmem(ndof, elems),
+        vmem(4, ndof, elems),
         vmem(*ints.shape),
         vmem(2, ndof, elems),
         vmem(2, ndof, elems),
@@ -548,8 +661,8 @@
         vmem(2, own_aggs, modes_n),
         vmem(own_aggs, modes_n),
         vmem(elems, modes_n),
-        vmem(parts, 1, elems),
-        vmem(parts, 1, elems),
+        vmem(2, count * PAIR, 1, elems),
+        vmem(2, 2 * X, 1, elems),
         vmem(count, 8, elems),
         dma((2,)),
         dma((2,)),
@@ -557,10 +670,11 @@
         dma((8,)),
         dma((4,)),
         dma((4,)),
-        dma((2,)),
-        dma((2,)),
+        dma((2, 2)),
+        dma((2, 2)),
         dma,
         dma,
+        dma((8,)),
     ]
     out, trace_tile = pl.pallas_call(
         functools.partial(kernel, parts, count),
@@ -568,11 +682,12 @@
             jax.ShapeDtypeStruct((2, ndof, elems), F32),
             jax.ShapeDtypeStruct((8, elems), F32),
         ),
-        in_specs=[pl.BlockSpec(memory_space=pltpu.VMEM)] * 10,
+        in_specs=[pl.BlockSpec(memory_space=pltpu.HBM)] * 9
+        + [pl.BlockSpec(memory_space=pltpu.VMEM)],
         out_specs=(pl.BlockSpec(memory_space=pltpu.VMEM),) * 2,
         scratch_shapes=scratch,
         compiler_params=pltpu.CompilerParams(
-            collective_id=0, has_side_effects=True, vmem_limit_bytes=48 * 1024 * 1024
+            collective_id=0, has_side_effects=True, vmem_limit_bytes=60 * 1024 * 1024
         ),
     )(
         probes,

time: 236 us -> 220 us (0.932)
  Pallas kernels: 223 us -> 214 us
  local copies, waits for them, and re-layouts: 11 us -> 4.34 us
    pallas_call x1, Pallas kernels: 223 us -> 214 us  [on_device(): pl.pallas_call(functools.partial(kernel, parts, count), out_shape=(jax.Sh...]
    unnamed x23 -> x5, local copies, waits for them, and re-layouts: 9.62 us -> 1.38 us
where the time goes in v3:
time: 220 us
  Pallas kernels  214 us (97%)
  local copies, waits for them, and re-layouts  4.34 us (2%)
    pallas_call x1, Pallas kernels, on_device(): pl.pallas_call(functools.partial(kernel, parts, count), out_shape=(jax.Sh...  214 us

profile of v3, /device:TPU:8, one launch (start us, length us, event | category | flops | bytes accessed | tf_op | source)
XLA Modules:
  0.0 219.5 jit_solution(7451435370041368654)
XLA Ops:
  0.6 0.1 pad.3.clone
  0.7 0.8 copy.16
  1.5 0.0 copy-start
  1.5 0.0 copy-start.1
  1.5 0.1 reshape.9
  1.6 0.6 copy-done
  2.2 0.0 copy-done.1
  2.2 0.7 add_convert_fusion.ints_in
  2.8 213.9 %shard_map.139 = (f32[2,192,128]{2,1,0:T(8,128)}, f32[8,128]{1,0:T(8,128)}) custom-call(f32[1,192,128]{2,1,0:T(8,128)} %probe_far.1, f32[192,128]{1,0:T(8,128)} %visc_far.1, f32[192,128]{1,0:T(8,128)} %fric_far.1, f32[192,128]{1,0:T(8,128)} %sens_far.1, f32[192,128]{1,0:T(8,128)} %misfit_far.1, f32[192,192]{1,0:T(8,128)} %grad_far.1, f32[192,192]{1,0:T(8,128)} %trace_far.1, ...), custom_call_target="tpu_custom_call" | custom-call | tf_op jit(solution)/shard_map/pallas_call | solution.py:679
  216.7 1.2 slice.11
  217.9 1.6 fusion
  (1 shorter events, 0.0 us)
Async XLA Ops:
  1.5 0.7 copy-start
  1.5 0.7 copy-start.1

commit v4 on v3

--- a/solution.py
+++ b/solution.py
@@ -65,7 +65,8 @@
     modes_far,
     inv_far,
     ints_in,
-    out,
+    first_out,
+    second_out,
     trace_out,
     probe_in,
     visc_in,
@@ -148,9 +149,10 @@
     leaf, core, along = lax.axis_index("leaf"), lax.axis_index("agg"), lax.axis_index("probe")
     z, x = lax.div(leaf, X), lax.rem(leaf, X)
     probe, low = lax.div(z, PAIR), lax.rem(z, PAIR)
-    unit = ((along * PAIR + low) * X + x) * 2 + core
-    mirror_leaf = (along * PAIR + low) * X + x
-    at_home = along == probe
+    quarter = lax.rem(along - probe + probes, probes)
+    unit = ((quarter * PAIR + low) * X + x) * 2 + core
+    at_home = along + probe == 0
+    in_place = quarter == probe
     ndof = grad.shape[0]
     elems = visc_in.shape[1]
     slots = parts * CAP
@@ -162,12 +164,14 @@
     xs = [lax.rem(x + step, X) for step in range(X)]
     cores = [core, 1 - core]
     alongs = [lax.rem(along + step, probes) for step in range(probes)]
+    quarters = [lax.rem(quarter + step, probes) for step in range(probes)]
     leaves = [[(probe * PAIR + part) * X + place for place in xs] for part in lows]
 
     def reached(step):
         y_step, z_step, x_step, core_step = step
         device = (leaves[z_step][x_step], cores[core_step], alongs[y_step])
-        peer = ((alongs[y_step] * PAIR + lows[z_step]) * X + xs[x_step]) * 2 + cores[core_step]
+        peer = (quarters[y_step] * PAIR + lows[z_step]) * X + xs[x_step]
+        peer = peer * 2 + cores[core_step]
         return device, peer
 
     steps = group_steps(probes)
@@ -185,7 +189,12 @@
         ((lax.rem(probe + step, probes) * PAIR + low) * X + x, core, along)
         for step in range(1, probes)
     ]
-    mirrors = [(mirror_leaf, side, probe) for side in cores]
+    away = (quarter * PAIR + low) * X + x
+    homes = [(away, side, probe) for side in cores]
+    workers = [
+        ((along * PAIR + low) * X + x, side, lax.rem(probe + along, probes)) for side in cores
+    ]
+    plane = (away, core, along)
 
     barrier = pltpu.get_barrier_semaphore()
     for device in [device for device, _ in peers] + mates:
@@ -193,43 +202,49 @@
 
     @pl.when(jnp.logical_not(at_home))
     def _():
-        for device in mirrors:
+        for device in homes + workers:
             pl.semaphore_signal(barrier, inc=1, device_id=device, device_id_type=MESH)
+
+    @pl.when(jnp.logical_not(in_place))
+    def _():
+        pl.semaphore_signal(barrier, inc=1, device_id=plane, device_id_type=MESH)
 
     def wait_bytes(ref, sem):
         pltpu.make_async_copy(ref, ref, sem).wait()
 
-    def mirror_start(source, target, send_at, recv_at, step=0):
+    def move_start(device, stays, source, target, send_at, recv_at):
         def remote():
-            return pltpu.make_async_remote_copy(
+            pltpu.make_async_remote_copy(
                 src_ref=source,
                 dst_ref=target,
                 send_sem=send_at,
                 recv_sem=recv_at,
-                device_id=mirrors[step],
+                device_id=device,
                 device_id_type=MESH,
-            )
-
-        if step:
-            remote().start()
+            ).start()
+
+        if stays is None:
+            remote()
         else:
 
-            @pl.when(at_home)
+            @pl.when(stays)
             def _():
                 pltpu.make_async_copy(source, target, recv_at).start()
 
-            @pl.when(jnp.logical_not(at_home))
+            @pl.when(jnp.logical_not(stays))
             def _():
-                remote().start()
-
-    def mirror_sent(source, send_at, step=0):
-        if step:
+                remote()
+
+    def move_sent(stays, source, send_at):
+        if stays is None:
             wait_bytes(source, send_at)
         else:
 
-            @pl.when(jnp.logical_not(at_home))
+            @pl.when(jnp.logical_not(stays))
             def _():
                 wait_bytes(source, send_at)
+
+    own_or_none = [at_home, None]
 
     rows = lax.broadcasted_iota(jnp.int32, (elems, elems), 0).astype(F32)
 
@@ -263,24 +278,36 @@
     def _():
         pl.semaphore_wait(barrier, others + probes - 1)
 
-    @pl.when(jnp.logical_not(at_home))
+    @pl.when(jnp.logical_and(in_place, jnp.logical_not(at_home)))
     def _():
-        pl.semaphore_wait(barrier, others + probes + 1)
+        pl.semaphore_wait(barrier, others + probes + 3)
+
+    @pl.when(jnp.logical_not(in_place))
+    def _():
+        pl.semaphore_wait(barrier, others + probes + 4)
 
     sources = [ints_in, home, visc_in, fric_in, misfit_far]
     targets = [ints] + [moved.at[which] for which in range(4)]
 
+    ways = [(plane, in_place), (workers[0], at_home)] + [(plane, in_place)] * 3
+
     def moved_start(which):
-        mirror_start(
-            sources[which], targets[which], move_send_sem.at[which], move_recv_sem.at[which]
+        device, stays = ways[which]
+        move_start(
+            device,
+            stays,
+            sources[which],
+            targets[which],
+            move_send_sem.at[which],
+            move_recv_sem.at[which],
         )
+
+    def moved_end(which):
+        wait_bytes(targets[which], move_recv_sem.at[which])
+        move_sent(ways[which][1], sources[which], move_send_sem.at[which])
 
     for which in range(4):
         moved_start(which)
-
-    def moved_end(which):
-        wait_bytes(targets[which], move_recv_sem.at[which])
-        mirror_sent(sources[which], move_send_sem.at[which])
 
     for slot, matrix in enumerate((grad[...].T, grad[...], trace[...].T, trace[...])):
         weights_h[slot], weights_l[slot] = split(matrix)
@@ -398,18 +425,19 @@
         projected = dot_split(residual, (modes_h[...], modes_l[...]))
         sums[...] = dot_exact(group_sum[...], split(projected))
         for step, side in enumerate(cores):
-            mirror_start(
+            move_start(
+                homes[step],
+                own_or_none[step],
                 sums.at[agg_rows(side)],
                 sums_in.at[step],
                 coarse_send_sem.at[step],
                 coarse_recv_sem.at[step],
-                step,
             )
 
     def coarse_solve():
         for step, side in enumerate(cores):
             wait_bytes(sums_in.at[step], coarse_recv_sem.at[step])
-            mirror_sent(sums.at[agg_rows(side)], coarse_send_sem.at[step], step)
+            move_sent(own_or_none[step], sums.at[agg_rows(side)], coarse_send_sem.at[step])
         total = sums_in[0] + sums_in[1]
         row = lax.broadcasted_iota(jnp.int32, total.shape, 0)
         result = jnp.zeros_like(total)
@@ -418,29 +446,29 @@
             result = jnp.where(row == block, one, result)
         solved_own[...] = result
         for step in range(2):
-            mirror_start(
+            move_start(
+                workers[step],
+                own_or_none[step],
                 solved_own,
                 solved.at[agg_rows(core)],
                 coarse_send_sem.at[2 + step],
                 coarse_recv_sem.at[2 + step],
-                step,
             )
 
     def coarse_end():
         for step, side in enumerate(cores):
             wait_bytes(solved.at[agg_rows(side)], coarse_recv_sem.at[2 + step])
-            mirror_sent(solved_own, coarse_send_sem.at[2 + step], step)
+            move_sent(own_or_none[step], solved_own, coarse_send_sem.at[2 + step])
         spread = dot_exact(group_spread[...], split(solved[...]))
         return dot_split(spread, (modes_t_h[...], modes_t_l[...]))
 
     def precondition(residual_ref, turn, started, later=None):
         def beside():
             started()
-            coarse_start(residual_ref[...])
+            coarse_solve()
 
         changed = operate(pre[...], turn, beside)
         pre[...] += (residual_ref[...] - changed) * inv_diag[...]
-        coarse_solve()
         changed = operate(pre[...], 1 - turn, later)
         pre[...] += (residual_ref[...] - changed) * inv_diag[...]
         return pre[...] + coarse_end()
@@ -454,7 +482,7 @@
         [step for step in steps if step[2:] == (0, 0)],
         [step for step in steps if step[:2] == (0, 0)],
     ]
-    stage_spots = [along * PAIR + low, x * 2 + core]
+    stage_spots = [quarter * PAIR + low, x * 2 + core]
     stage_buffers = [dots_a, dots_b]
 
     def dots_send(which, stage, row):
@@ -504,11 +532,17 @@
                 start = pre[...] / inv_diag[...]
                 probe_sens[...] = start
                 rhs[...] = start
+                coarse_start(start)
                 moved_start(4)
+
+        @pl.when(solve != 0)
+        def _():
+            coarse_start(rhs[...])
 
         first_dir[...] = precondition(rhs, 0, first_time)
         image[...] = operate(first_dir[...], 0)
         pre[...] = image[...] * inv_diag[...]
+        coarse_start(image[...])
 
         def sums_first():
             dots_start(
@@ -547,7 +581,9 @@
         weight_first = step + step_next * ratio
         result = weight_first * first_dir[...] + step_next * pre[...]
         result_out[solve] = result.T
-        mirror_start(
+        move_start(
+            homes[0],
+            at_home,
             result_out.at[solve],
             result_in.at[solve],
             move_send_sem.at[6 + solve],
@@ -571,9 +607,9 @@
         ).start()
     for solve in range(2):
         wait_bytes(result_in.at[solve], move_recv_sem.at[6 + solve])
-        mirror_sent(result_out.at[solve], move_send_sem.at[6 + solve])
-    out[0] = result_in[0]
-    out[1] = result_in[1] * sens_in[...]
+        move_sent(at_home, result_out.at[solve], move_send_sem.at[6 + solve])
+    first_out[0] = result_in[0]
+    second_out[0] = result_in[1] * sens_in[...]
     blocks = traces_all.at[pl.ds(0, probes - 1)]
     wait_bytes(blocks, last_recv_sem)
     wait_bytes(blocks, last_send_sem)
@@ -676,15 +712,17 @@
         dma,
         dma((8,)),
     ]
-    out, trace_tile = pl.pallas_call(
+    field_out = jax.ShapeDtypeStruct((1, ndof, elems), F32)
+    first, second, trace_tile = pl.pallas_call(
         functools.partial(kernel, parts, count),
         out_shape=(
-            jax.ShapeDtypeStruct((2, ndof, elems), F32),
+            field_out,
+            field_out,
             jax.ShapeDtypeStruct((8, elems), F32),
         ),
         in_specs=[pl.BlockSpec(memory_space=pltpu.HBM)] * 9
         + [pl.BlockSpec(memory_space=pltpu.VMEM)],
-        out_specs=(pl.BlockSpec(memory_space=pltpu.VMEM),) * 2,
+        out_specs=(pl.BlockSpec(memory_space=pltpu.VMEM),) * 3,
         scratch_shapes=scratch,
         compiler_params=pltpu.CompilerParams(
             collective_id=0, has_side_effects=True, vmem_limit_bytes=60 * 1024 * 1024
@@ -701,7 +739,7 @@
         coarse_inv,
         ints,
     )
-    return out[0][None], out[1][None], trace_tile[0, 0]
+    return first, second, trace_tile[0, 0]
 
 
 def solution(mesh):

time: 220 us -> 206 us (0.936)
  Pallas kernels: 214 us -> 199 us
    pallas_call x1, Pallas kernels: 214 us -> 199 us  [on_device(): pl.pallas_call(functools.partial(kernel, parts, count), out_shape=(field_...]
    unnamed x5 -> x9, local copies, waits for them, and re-layouts: 1.38 us -> 3.59 us
where the time goes in v4:
time: 206 us
  Pallas kernels  199 us (97%)
  local copies, waits for them, and re-layouts  4.93 us (2%)
    pallas_call x1, Pallas kernels, on_device(): pl.pallas_call(functools.partial(kernel, parts, count), out_shape=(field_...  199 us

profile of v4, /device:TPU:8, one launch (start us, length us, event | category | flops | bytes accessed | tf_op | source)
XLA Modules:
  0.0 205.5 jit_solution(6125276597697080538)
XLA Ops:
  0.6 0.1 pad.3.clone
  0.7 0.8 copy.16
  1.5 0.0 copy-start.1
  1.5 0.0 copy-start.2
  1.5 0.1 reshape.9
  1.6 0.6 copy-done.1
  2.2 0.0 copy-done.2
  2.2 0.7 add_convert_fusion.ints_in
  2.8 199.2 %shard_map.139 = (f32[1,192,128]{2,1,0:T(8,128)}, f32[1,192,128]{2,1,0:T(8,128)}, f32[8,128]{1,0:T(8,128)}) custom-call(f32[1,192,128]{2,1,0:T(8,128)} %probe_far.1, f32[192,128]{1,0:T(8,128)} %visc_far.1, f32[192,128]{1,0:T(8,128)} %fric_far.1, f32[192,128]{1,0:T(8,128)} %sens_far.1, f32[192,128]{1,0:T(8,128)} %misfit_far.1, f32[192,192]{1,0:T(8,128)} %grad_far.1, ...), custom_call_target="tpu_custom_call" | custom-call | tf_op jit(solution)/shard_map/pallas_call | solution.py:716
  202.1 1.2 slice.3
  203.3 0.0 copy-start
  203.3 1.6 copy.19
  204.9 0.0 copy-done
  204.9 0.6 copy.20
  (1 shorter events, 0.0 us)
Async XLA Ops:
  1.5 0.7 copy-start.1
  1.5 0.7 copy-start.2
  203.3 1.6 copy-start

commit v5 on v4

--- a/solution.py
+++ b/solution.py
@@ -29,6 +29,12 @@
 
 def dot_exact(left, right_pair):
     return dot(left, right_pair[0]) + dot(left, right_pair[1])
+
+
+def dot_wide(left, right):
+    width = right.shape[1]
+    both = dot(left, jnp.concatenate(split(right), 1))
+    return both[:, :width] + both[:, width:]
 
 
 def dot_split(left, right_pair):
@@ -325,7 +331,8 @@
         here = pl.ds(block * elems, elems)
         scatter[:, here] = hot.astype(BF16)
         hot_t = hot.T
-        gather[here, :] = hot_t.astype(BF16)
+        gather[here, :elems] = hot_t.astype(BF16)
+        gather[here, elems:] = hot_t.astype(BF16)
         paired = hot_t.reshape(elems // CAP, 2, halves, elems)
         half = pl.ds(block * (elems // 2), elems // 2)
         gather_two[half, :elems] = paired[:, 0].reshape(elems // 2, elems).astype(BF16)
@@ -355,9 +362,8 @@
         traced = dot_split(value, weight(2))
         high, low_part = split(traced)
         blank = jnp.zeros((elems, rest), BF16)
-        send[turn, :, :CAP, :] = dot_exact(
-            gather[...], (high[:, :elems], low_part[:, :elems])
-        ).reshape(parts, CAP, elems)
+        both = jnp.concatenate([high[:, :elems], low_part[:, :elems]], 0)
+        send[turn, :, :CAP, :] = dot(gather[...], both).reshape(parts, CAP, elems)
 
         def two(piece):
             tail = piece[:, elems:]
@@ -406,10 +412,8 @@
         near = count[...] * traced - dot_exact(adjacent[...], (high, low_part))
         inner = inner + fric[...] * value
         wait_blocks(turn, recv_sem)
-        first = dot_exact(scatter[...], split(recv[turn, :, :CAP, :].reshape(slots, elems)))
-        second = dot_exact(
-            scatter_two[...], split(recv[turn, :, CAP:, :].reshape(slots // 2, elems))
-        )
+        first = dot_wide(scatter[...], recv[turn, :, :CAP, :].reshape(slots, elems))
+        second = dot_wide(scatter_two[...], recv[turn, :, CAP:, :].reshape(slots // 2, elems))
         second = second[:elems, :rest] + second[elems:, rest:]
         near = near - jnp.concatenate([first, second], 1)
         result = inner + dot_split(near, weight(3))
@@ -669,7 +673,7 @@
         vmem(own_aggs, modes_n, modes_n, dtype=BF16),
         vmem(elems, slots, dtype=BF16),
         vmem(2 * elems, slots // 2, dtype=BF16),
-        vmem(slots, elems, dtype=BF16),
+        vmem(slots, 2 * elems, dtype=BF16),
         vmem(slots // 2, 2 * elems, dtype=BF16),
         vmem(elems, elems, dtype=BF16),
         vmem(aggs * own_aggs, elems, dtype=BF16),

time: 206 us -> 204 us (level)
  no operation moved by 1% of the time
where the time goes in v5:
time: 204 us
  Pallas kernels  198 us (97%)
  local copies, waits for them, and re-layouts  4.93 us (2%)
    pallas_call x1, Pallas kernels, on_device(): pl.pallas_call(functools.partial(kernel, parts, count), out_shape=(field_...  198 us

profile of v5, /device:TPU:8, one launch (start us, length us, event | category | flops | bytes accessed | tf_op | source)
XLA Modules:
  0.0 204.0 jit_solution(15961541711970022859)
XLA Ops:
  0.6 0.1 pad.3.clone
  0.7 0.8 copy.16
  1.5 0.0 copy-start.1
  1.5 0.0 copy-start.2
  1.5 0.1 reshape.9
  1.6 0.6 copy-done.1
  2.2 0.0 copy-done.2
  2.2 0.7 add_convert_fusion.ints_in
  2.8 197.8 %shard_map.139 = (f32[1,192,128]{2,1,0:T(8,128)}, f32[1,192,128]{2,1,0:T(8,128)}, f32[8,128]{1,0:T(8,128)}) custom-call(f32[1,192,128]{2,1,0:T(8,128)} %probe_far.1, f32[192,128]{1,0:T(8,128)} %visc_far.1, f32[192,128]{1,0:T(8,128)} %fric_far.1, f32[192,128]{1,0:T(8,128)} %sens_far.1, f32[192,128]{1,0:T(8,128)} %misfit_far.1, f32[192,192]{1,0:T(8,128)} %grad_far.1, ...), custom_call_target="tpu_custom_call" | custom-call | tf_op jit(solution)/shard_map/pallas_call | solution.py:720
  200.6 1.2 slice.3
  201.8 0.0 copy-start
  201.8 1.6 copy.19
  203.4 0.0 copy-done
  203.4 0.6 copy.20
  (1 shorter events, 0.0 us)
Async XLA Ops:
  1.5 0.7 copy-start.1
  1.5 0.7 copy-start.2
  201.8 1.6 copy-start

commit v6 on v5

--- a/solution.py
+++ b/solution.py
@@ -71,8 +71,7 @@
     modes_far,
     inv_far,
     ints_in,
-    first_out,
-    second_out,
+    out,
     trace_out,
     probe_in,
     visc_in,
@@ -612,8 +611,8 @@
     for solve in range(2):
         wait_bytes(result_in.at[solve], move_recv_sem.at[6 + solve])
         move_sent(at_home, result_out.at[solve], move_send_sem.at[6 + solve])
-    first_out[0] = result_in[0]
-    second_out[0] = result_in[1] * sens_in[...]
+    out[0] = result_in[0]
+    out[1] = result_in[1] * sens_in[...]
     blocks = traces_all.at[pl.ds(0, probes - 1)]
     wait_bytes(blocks, last_recv_sem)
     wait_bytes(blocks, last_send_sem)
@@ -716,17 +715,15 @@
         dma,
         dma((8,)),
     ]
-    field_out = jax.ShapeDtypeStruct((1, ndof, elems), F32)
-    first, second, trace_tile = pl.pallas_call(
+    out, trace_tile = pl.pallas_call(
         functools.partial(kernel, parts, count),
         out_shape=(
-            field_out,
-            field_out,
+            jax.ShapeDtypeStruct((2, ndof, elems), F32),
             jax.ShapeDtypeStruct((8, elems), F32),
         ),
         in_specs=[pl.BlockSpec(memory_space=pltpu.HBM)] * 9
         + [pl.BlockSpec(memory_space=pltpu.VMEM)],
-        out_specs=(pl.BlockSpec(memory_space=pltpu.VMEM),) * 3,
+        out_specs=(pl.BlockSpec(memory_space=pltpu.VMEM),) * 2,
         scratch_shapes=scratch,
         compiler_params=pltpu.CompilerParams(
             collective_id=0, has_side_effects=True, vmem_limit_bytes=60 * 1024 * 1024
@@ -743,7 +740,7 @@
         coarse_inv,
         ints,
     )
-    return first, second, trace_tile[0, 0]
+    return out[0][None], out[1][None], trace_tile[0, 0]
 
 
 def solution(mesh):

time: 204 us -> 204 us (level)
    unnamed x9 -> x5, local copies, waits for them, and re-layouts: 3.59 us -> 1.38 us
where the time goes in v6:
time: 204 us; the launch traced here: 203 us
  Pallas kernels  198 us (97%)
  local copies, waits for them, and re-layouts  4.34 us (2%)
    pallas_call x1, Pallas kernels, on_device(): pl.pallas_call(functools.partial(kernel, parts, count), out_shape=(jax.Sh...  198 us

profile of v6, /device:TPU:8, one launch (start us, length us, event | category | flops | bytes accessed | tf_op | source)
XLA Modules:
  0.0 203.4 jit_solution(13374724599553591144)
XLA Ops:
  0.6 0.1 pad.3.clone
  0.7 0.8 copy.16
  1.5 0.0 copy-start
  1.5 0.0 copy-start.1
  1.5 0.1 reshape.9
  1.6 0.6 copy-done
  2.2 0.0 copy-done.1
  2.2 0.7 add_convert_fusion.ints_in
  2.8 197.8 %shard_map.139 = (f32[2,192,128]{2,1,0:T(8,128)}, f32[8,128]{1,0:T(8,128)}) custom-call(f32[1,192,128]{2,1,0:T(8,128)} %probe_far.1, f32[192,128]{1,0:T(8,128)} %visc_far.1, f32[192,128]{1,0:T(8,128)} %fric_far.1, f32[192,128]{1,0:T(8,128)} %sens_far.1, f32[192,128]{1,0:T(8,128)} %misfit_far.1, f32[192,192]{1,0:T(8,128)} %grad_far.1, f32[192,192]{1,0:T(8,128)} %trace_far.1, ...), custom_call_target="tpu_custom_call" | custom-call | tf_op jit(solution)/shard_map/pallas_call | solution.py:718
  200.6 1.2 slice.11
  201.8 1.6 fusion
  (1 shorter events, 0.0 us)
Async XLA Ops:
  1.5 0.7 copy-start
  1.5 0.7 copy-start.1
